TPU v7x, 256 devices: a whole 4x4x8 slice. The times are simulated.
256 devices in a mesh: rep: 8 (over y, core), dom: 32 (over z, x).
Axes of the slice: x: 4, y: 4, z: 8, core: 2. Of those that a mesh axis runs over, the one named last changes fastest.
Arguments:
- tile_values: bfloat16 [8, 32, 32, 2, 128, 128], P('rep', 'dom'), may hold values from -0.09375 to 0.09375
- tile_rows: int32 [8, 32, 32, 2], P('rep', 'dom'), may hold values from 0 to 1
- tile_cols: int32 [8, 32, 32, 2], P('rep', 'dom'), may hold values from 0 to 15
- tile_counts: int32 [8, 32, 32], P('rep', 'dom'), may hold values from 0 to 2
- features: bfloat16 [65536, 128], P(('dom', 'rep')), may hold values from -6 to 6
- weight_in: bfloat16 [128, 512], replicated, may hold values from -0.5 to 0.5
- weight_out: bfloat16 [512, 512], replicated, may hold values from -0.25 to 0.25
- cotangent: bfloat16 [65536, 512], P(('dom', 'rep')), may hold values from -0.0234375 to 0.0234375
Outputs:
- logits: bfloat16 [65536, 512], P(('dom', 'rep'))
- grad_in: float32 [128, 512], replicated
- grad_out: float32 [512, 512], replicated
Inputs may be any that keep to these rules, and one draw needn't show every extreme that they name: `tile_counts`: slots at or after the count hold values that are not used.
All inputs are finite; a program needn't handle non-finite values.
Results may differ from a plain program's by a relative error of at most 0.018.
Values may be sent and summed in bfloat16 or wider, within the bound.
A program may use at most 128 MiB of HBM per device.

v0:
```python
import jax
import jax.numpy as jnp
from jax import lax
from jax.sharding import PartitionSpec as P


def silu_slope(value):
    sig = jax.nn.sigmoid(value)
    return sig * (1.0 + value * (1.0 - sig))


def route(values):
    return lax.all_to_all(values, "dom", split_axis=0, concat_axis=0, tiled=True)


def per_device(
    tile_values, tile_rows, tile_cols, tile_counts, features, weight_in, weight_out, cotangent
):
    tiles = tile_values[0, 0]
    rows = tile_rows[0, 0]
    cols = tile_cols[0, 0]
    counts = tile_counts[0, 0]
    width = tiles.shape[-1]
    slots = tiles.shape[1]
    node_rows = features.shape[0]
    row_blocks = node_rows // width
    col_blocks = lax.axis_size("rep") * node_rows // width
    live = jnp.arange(slots)[None, :] < counts[:, None]
    tiles = jnp.where(live[:, :, None, None], tiles, jnp.zeros_like(tiles))
    row_table = (rows[:, :, None] == jnp.arange(row_blocks)[None, None, :]).astype(jnp.bfloat16)
    far_cols = lax.all_to_all(cols, "dom", split_axis=0, concat_axis=0, tiled=True)
    col_table = (far_cols[:, :, None] == jnp.arange(col_blocks)[None, None, :]).astype(jnp.bfloat16)
    far_tiles = lax.all_to_all(tiles, "dom", split_axis=0, concat_axis=0, tiled=True)

    def aggregate(values):
        block = lax.all_gather(values, "rep", axis=0, tiled=True)
        blocks = block.reshape(col_blocks, width, values.shape[1])
        picked = blocks[far_cols]
        prod = jnp.einsum("sktu,skuf->sktf", far_tiles, picked, preferred_element_type=jnp.float32)
        ready = route(prod.astype(jnp.bfloat16))
        summed = jnp.einsum("skb,sktf->btf", row_table, ready, preferred_element_type=jnp.float32)
        return summed.reshape(node_rows, values.shape[1]).astype(jnp.bfloat16)

    agg1 = aggregate(features)
    z1 = jnp.dot(agg1, weight_in, preferred_element_type=jnp.float32)
    hidden = jax.nn.silu(z1).astype(jnp.bfloat16)
    agg2 = aggregate(hidden)
    logits = jnp.dot(agg2, weight_out, preferred_element_type=jnp.float32).astype(jnp.bfloat16)
    contract = (((1,), (1,)), ((), ()))
    dagg = lax.dot_general(
        cotangent, weight_out, contract, preferred_element_type=jnp.float32
    ).astype(jnp.bfloat16)
    mine = dagg.reshape(row_blocks, width, dagg.shape[1])[rows]
    arrived = route(mine)
    terms = jnp.einsum(
        "sktu,sktf->skuf", far_tiles, arrived, preferred_element_type=jnp.float32
    ).astype(jnp.bfloat16)
    partial_sum = jnp.einsum("skc,skuf->cuf", col_table, terms, preferred_element_type=jnp.float32)
    partial_sum = partial_sum.reshape(col_blocks * width, dagg.shape[1])
    dh = lax.psum_scatter(
        partial_sum.astype(jnp.bfloat16), "rep", scatter_dimension=0, tiled=True
    ).astype(jnp.float32)
    dz = (dh * silu_slope(z1)).astype(jnp.bfloat16)
    over_rows = (((0,), (0,)), ((), ()))
    term_in = lax.dot_general(agg1, dz, over_rows, preferred_element_type=jnp.float32)
    term_out = lax.dot_general(agg2, cotangent, over_rows, preferred_element_type=jnp.float32)
    grad_in, grad_out = lax.psum((term_in, term_out), ("rep", "dom"))
    return (logits, grad_in, grad_out)


def solution(mesh):
    placed = (
        P("rep", "dom", None, None, None, None),
        P("rep", "dom", None, None),
        P("rep", "dom", None, None),
        P("rep", "dom", None),
        P(("dom", "rep"), None),
        P(),
        P(),
        P(("dom", "rep"), None),
    )
    return jax.shard_map(
        per_device,
        mesh=mesh,
        in_specs=placed,
        out_specs=(P(("dom", "rep"), None), P(), P()),
        check_vma=False,
    )
```

profile of v0, /device:TPU:1, one launch (start us, length us, event | category | flops | bytes accessed | tf_op | source)
XLA Modules:
  0.0 805.5 jit_solution(13561644297094570303)
XLA Ops:
  7.2 0.0 copy-start
  7.2 1.4 copy.19
  8.6 11.9 %all-to-all-start.1 = ((s32[32,1,2]{2,1,0:T(1,128)}), s32[32,1,2]{2,1,0:T(1,128)S(1)}, u32[]{:S(2)}, u32[]{:S(2)}) async-start(s32[32,1,2]{2,1,0:T(1,128)} %copy.19), calls=%async_computation.1 | async-start | bytes 32768 | tf_op jit(solution)/shard_map/all_to_all | solution.py:31
  20.5 0.7 iota_compare_fusion.1
  21.2 3.1 bitcast_select_fusion
  24.3 0.0 copy-start.2
  24.3 4.6 all-to-all-done.1
  29.0 4.7 all-to-all-start
  33.7 0.0 copy-done.2
  33.7 15.0 %all_gather.6 = bf16[2048,128]{1,0:T(8,128)(2,1)S(1)} all-gather(bf16[256,128]{1,0:T(8,128)(2,1)S(1)} %copy-done.2), channel_id=1, replica_groups=mesh['rep'=8,'dom'=32] {'rep'}, dimensions={0}, use_global_device_ids=true | all-gather | bytes 589824 | tf_op jit(solution)/shard_map/all_gather | solution.py:36
  48.7 0.1 copy.20
  48.8 0.1 copy.21
  48.9 0.1 reshape.112
  49.0 2.1 gather_fusion
  51.1 30.5 %all-to-all-done = bf16[32,2,128,128]{3,2,1,0:T(8,128)(2,1)S(1)} async-done(((bf16[32,2,128,128]{3,2,1,0:T(8,128)(2,1)}), bf16[32,2,128,128]{3,2,1,0:T(8,128)(2,1)S(1)}, u32[]{:S(2)}, u32[]{:S(2)}) %all-to-all-start) | async-done | bytes 2097184 | tf_op jit(solution)/shard_map/all_to_all | solution.py:33
  81.7 2.3 convolution_convert_fusion.2
  83.9 3.5 copy.22
  87.5 0.0 copy-start.3
  87.5 0.0 copy-start.1
  87.5 6.9 all-to-all-start.2
  94.4 0.0 copy-done.3
  94.4 0.1 copy.29
  94.5 0.1 reshape.128
  94.6 0.0 copy-done
  94.6 0.0 copy-done.1
  94.6 0.3 convolution_convert_fusion.3
  95.0 5.4 gather_fusion.2
  100.4 40.1 %all-to-all-done.2 = bf16[32,2,128,128]{3,1,2,0:T(2,128)(2,1)} async-done(((bf16[32,2,128,128]{3,1,2,0:T(2,128)(2,1)}), bf16[32,2,128,128]{3,1,2,0:T(2,128)(2,1)}, u32[]{:S(2)}, u32[]{:S(2)}) %all-to-all-start.2) | async-done | bytes 2097184 | tf_op jit(solution)/shard_map/all_to_all | solution.py:13
  140.4 7.6 all-to-all-start.4
  148.1 0.0 copy-start.4
  148.1 0.2 all-gather.2.cloned.1.call-start
  148.3 2.9 fusion.17
  151.2 0.0 copy-done.4
  151.2 1.1 multiply_convert_fusion.1
  152.3 0.0 all-gather.2.cloned.1.call-update
  152.3 32.5 %all-gather.2.cloned.1.call-done = bf16[2048,512]{1,0:T(8,128)(2,1)} async-done(((bf16[256,512]{1,0:T(8,128)(2,1)}), bf16[2048,512]{1,0:T(8,128)(2,1)}) %all-gather.2.cloned.1.call-update) | async-done | bytes 2097168 | tf_op jit(solution)/shard_map/all_gather | solution.py:36
  184.8 7.1 gather_fusion.1
  191.9 5.7 convolution_convert_fusion.1
  197.6 7.8 copy.25
  205.4 121.4 %all-to-all-done.4 = bf16[32,2,128,512]{3,2,1,0:T(8,128)(2,1)} async-done(((bf16[32,2,128,512]{3,2,1,0:T(8,128)(2,1)}), bf16[32,2,128,512]{3,2,1,0:T(8,128)(2,1)}, u32[]{:S(2)}, u32[]{:S(2)}) %all-to-all-start.4) | async-done | bytes 8388640 | tf_op jit(solution)/shard_map/all_to_all | solution.py:13
  326.8 12.0 %all-to-all-start.3 = ((bf16[32,2,128,512]{3,1,2,0:T(2,128)(2,1)}), bf16[32,2,128,512]{3,1,2,0:T(2,128)(2,1)}, u32[]{:S(2)}, u32[]{:S(2)}) async-start(bf16[32,2,128,512]{3,1,2,0:T(2,128)(2,1)} %copy.25), calls=%async_computation.3 | async-start | bytes 16777216 | tf_op jit(solution)/shard_map/all_to_all | solution.py:13
  338.8 0.3 reduce-scatter.2.cloned.1.call-start
  339.1 5.8 convolution_convert_fusion
  344.9 8.9 %bitcast_convert_fusion = bf16[16,128,512]{2,0,1:T(8,128)(2,1)S(1)} fusion(bf16[32,2,128,512]{3,2,1,0:T(8,128)(2,1)S(1)} %convolution_convert_fusion, s32[32,2]{0,1:T(2,128)S(1)} %bitcast.70), kind=kOutput, calls=%fused_computation.9 | convolution fusion | flops 135267328 | bytes 10486016 | tf_op jit(solution)/shard_map/skc,skuf->cuf/dot_general | solution.py:58
  353.8 2.8 copy.32
  356.6 0.0 copy-start.5
  356.6 0.0 reduce-scatter.2.cloned.1.call-update
  356.6 0.0 all-reduce.3.cloned.1.call-start
  356.6 37.1 %reduce-scatter.2.cloned.1.call-done = bf16[256,512]{1,0:T(8,128)(2,1)} async-done(((bf16[2048,512]{1,0:T(8,128)(2,1)}), bf16[256,512]{1,0:T(8,128)(2,1)}) %reduce-scatter.2.cloned.1.call-update) | async-done | bytes 262160 | tf_op jit(solution)/shard_map/reduce_scatter | solution.py:60
  393.7 0.0 copy-done.5
  393.7 2.0 fusion.20
  395.7 133.2 %all-to-all-done.3 = bf16[32,2,128,512]{3,1,2,0:T(2,128)(2,1)} async-done(((bf16[32,2,128,512]{3,1,2,0:T(2,128)(2,1)}), bf16[32,2,128,512]{3,1,2,0:T(2,128)(2,1)}, u32[]{:S(2)}, u32[]{:S(2)}) %all-to-all-start.3) | async-done | bytes 8388640 | tf_op jit(solution)/shard_map/all_to_all | solution.py:13
  528.9 8.1 %fusion.11 = bf16[2,128,512]{2,0,1:T(2,128)(2,1)S(1)} fusion(bf16[32,2,128,512]{3,1,2,0:T(2,128)(2,1)} %all-to-all-done.3, s32[32,2]{0,1:T(2,128)S(1)} %bitcast.73), kind=kOutput, calls=%fused_computation.15 | convolution fusion | flops 16908416 | bytes 8651008 | tf_op jit(solution)/shard_map/skb,sktf->btf/dot_general | solution.py:41
  537.0 1.3 fusion.29
  538.3 0.0 all-reduce.3.cloned.1.call-update
  538.3 1.0 convolution_convert_fusion.4
  539.4 255.7 %all-reduce.3.cloned.1.call-done = (f32[128,512]{1,0:T(8,128)}, f32[512,512]{1,0:T(8,128)}) async-done(((f32[128,512]{1,0:T(8,128)}, f32[512,512]{1,0:T(8,128)}), (f32[128,512]{1,0:T(8,128)}, f32[512,512]{1,0:T(8,128)})) %all-reduce.3.cloned.1.call-update) | async-done | bytes 1310736 | tf_op jit(solution)/shard_map/psum | solution.py:67
  795.0 1.7 copy.55
  796.7 2.3 copy.56
  (6 shorter events, 0.1 us)
Async XLA Ops:
  7.2 87.5 %copy-start = (bf16[512,512]{1,0:T(8,128)(2,1)S(1)}, bf16[512,512]{1,0:T(8,128)(2,1)}, u32[]{:S(2)}) copy-start(bf16[512,512]{1,0:T(8,128)(2,1)} %param.14) | copy-start | bytes 1572868
  8.6 20.4 %all-to-all-start.1 = ((s32[32,1,2]{2,1,0:T(1,128)}), s32[32,1,2]{2,1,0:T(1,128)S(1)}, u32[]{:S(2)}, u32[]{:S(2)}) async-start(s32[32,1,2]{2,1,0:T(1,128)} %copy.19), calls=%async_computation.1 | async-start | bytes 32768 | tf_op jit(solution)/shard_map/all_to_all | solution.py:31
  24.3 9.4 %copy-start.2 = (bf16[256,128]{1,0:T(8,128)(2,1)S(1)}, bf16[256,128]{1,0:T(8,128)(2,1)}, u32[]{:S(2)}) copy-start(bf16[256,128]{1,0:T(8,128)(2,1)} %param.12) | copy-start | bytes 196612
  29.0 52.7 %all-to-all-start = ((bf16[32,2,128,128]{3,2,1,0:T(8,128)(2,1)}), bf16[32,2,128,128]{3,2,1,0:T(8,128)(2,1)S(1)}, u32[]{:S(2)}, u32[]{:S(2)}) async-start(bf16[32,2,128,128]{3,2,1,0:T(8,128)(2,1)} %bitcast_select_fusion), calls=%async_computation | async-start | bytes 4194304 | tf_op jit(solution)/shard_map/all_to_all | solution.py:33
  87.5 6.9 copy-start.3
  87.5 7.2 copy-start.1
  87.5 53.0 %all-to-all-start.2 = ((bf16[32,2,128,128]{3,1,2,0:T(2,128)(2,1)}), bf16[32,2,128,128]{3,1,2,0:T(2,128)(2,1)}, u32[]{:S(2)}, u32[]{:S(2)}) async-start(bf16[32,2,128,128]{3,1,2,0:T(2,128)(2,1)} %copy.22), calls=%async_computation.2 | async-start | bytes 4194304 | tf_op jit(solution)/shard_map/all_to_all | solution.py:13
  140.4 186.3 %all-to-all-start.4 = ((bf16[32,2,128,512]{3,2,1,0:T(8,128)(2,1)}), bf16[32,2,128,512]{3,2,1,0:T(8,128)(2,1)}, u32[]{:S(2)}, u32[]{:S(2)}) async-start(bf16[32,2,128,512]{3,2,1,0:T(8,128)(2,1)} %bitcast.62), calls=%async_computation.4 | async-start | bytes 16777216 | tf_op jit(solution)/shard_map/all_to_all | solution.py:13
  148.1 3.1 copy-start.4
  148.1 36.7 %all-gather.2.cloned.1.call-start = ((), (), s32[]{:S(2)}) async-start(), calls=%async_computation.6 | async-start | bytes 2359296 | tf_op jit(solution)/shard_map/all_gather | solution.py:36
  326.8 202.1 %all-to-all-start.3 = ((bf16[32,2,128,512]{3,1,2,0:T(2,128)(2,1)}), bf16[32,2,128,512]{3,1,2,0:T(2,128)(2,1)}, u32[]{:S(2)}, u32[]{:S(2)}) async-start(bf16[32,2,128,512]{3,1,2,0:T(2,128)(2,1)} %copy.25), calls=%async_computation.3 | async-start | bytes 16777216 | tf_op jit(solution)/shard_map/all_to_all | solution.py:13
  338.8 54.9 %reduce-scatter.2.cloned.1.call-start = ((), (), s32[]{:S(2)}) async-start(), calls=%async_computation.7 | async-start | bytes 2359296 | tf_op jit(solution)/shard_map/reduce_scatter | solution.py:60
  356.6 37.1 %copy-start.5 = (f32[256,512]{1,0:T(8,128)S(1)}, f32[256,512]{1,0:T(8,128)}, u32[]{:S(2)}) copy-start(f32[256,512]{1,0:T(8,128)} %get-tuple-element.6) | copy-start | bytes 1572868
  356.6 438.5 %all-reduce.3.cloned.1.call-start = ((), (), s32[]{:S(2)}) async-start(), calls=%async_computation.8 | async-start | bytes 2621440 | tf_op jit(solution)/shard_map/psum | solution.py:67
Sparse Core Ops, SparseCore 0:
  152.4 32.2 all-gather.1
  356.7 36.9 reduce-scatter.1
  538.5 256.5 all-reduce.2
where the time goes:
time: 807 us; the launch traced here: 806 us
  waiting for transfers between devices  655 us (81%)
  starting transfers between devices  43.7 us (5%)
  matrix products  39.3 us (5%)
  local copies, waits for them, and re-layouts  34.6 us (4%)
  blocking collectives  15 us (2%)
  between operations  13.9 us (2%)
    all_to_all x3, waiting for transfers between devices, route(): lax.all_to_all(values, 'dom', split_axis=0, concat_axis=0, tiled=True)  295 us
    psum x1, waiting for transfers between devices, per_device(): grad_in, grad_out = lax.psum((term_in, term_out), ('rep', 'dom'))  256 us
    reduce_scatter x1, waiting for transfers between devices, per_device(): lax.psum_scatter(partial_sum.astype(jnp.bfloat16), 'rep', scatter_dimensi...  37.1 us
    all_gather x1, waiting for transfers between devices, aggregate(): block = lax.all_gather(values, 'rep', axis=0, tiled=True)  32.5 us
    all_to_all x1, waiting for transfers between devices, per_device(): lax.all_to_all(tiles, 'dom', split_axis=0, concat_axis=0, tiled=True)  30.5 us
    all_to_all x3, starting transfers between devices, route(): lax.all_to_all(values, 'dom', split_axis=0, concat_axis=0, tiled=True)  26.6 us
  transfers between devices with their start and end apart: 8, of which 8 were waited for; matrix products, arithmetic and copies ran while one was open for 7% of the time, Pallas kernels for 0%

commit v1 on v0

v1 whole, which is shorter than its diff:
```python
import jax
import jax.numpy as jnp
from jax import lax
from jax.sharding import PartitionSpec as P


def route(values):
    return lax.all_to_all(values, "dom", split_axis=0, concat_axis=0, tiled=True)


def dot(a, b, ca, cb):
    return lax.dot_general(a, b, (((ca,), (cb,)), ((), ())), preferred_element_type=jnp.float32)


def per_device(
    tile_values, tile_rows, tile_cols, tile_counts, features, weight_in, weight_out, cotangent
):
    tiles = tile_values[0, 0]
    rows = tile_rows[0, 0]
    cols = tile_cols[0, 0]
    counts = tile_counts[0, 0]
    width = tiles.shape[-1]
    slots = tiles.shape[1]
    node_rows = features.shape[0]
    row_blocks = node_rows // width
    col_blocks = lax.axis_size("rep") * node_rows // width
    live = jnp.arange(slots)[None, :] < counts[:, None]
    here = live[None] & (rows[None] == jnp.arange(row_blocks)[:, None, None])
    spread = jnp.where(here[:, :, :, None, None], tiles[None], jnp.zeros_like(tiles)[None])
    spread = jnp.transpose(spread, (0, 3, 1, 2, 4)).reshape(node_rows, -1)
    far_cols = route(cols)

    def fetch(values):
        block = lax.all_gather(values, "rep", axis=0, tiled=True)
        picked = block.reshape(col_blocks, width, values.shape[1])[far_cols]
        return route(picked).reshape(-1, values.shape[1])

    agg1 = dot(spread, fetch(features), 1, 0).astype(jnp.bfloat16)
    near = fetch(agg1)
    z1 = dot(near, weight_in, 1, 0)
    sig = 0.5 + 0.5 * jnp.tanh(0.5 * z1)
    hidden = z1 * sig
    slope = sig + hidden * (1.0 - sig)
    agg2 = dot(spread, hidden.astype(jnp.bfloat16), 1, 0).astype(jnp.bfloat16)
    logits = dot(agg2, weight_out, 1, 0).astype(jnp.bfloat16)
    dagg = dot(cotangent, weight_out, 1, 1).astype(jnp.bfloat16)
    dz = (dot(spread, dagg, 0, 0) * slope).astype(jnp.bfloat16)
    term_in = dot(near, dz, 0, 0)
    term_out = dot(agg2, cotangent, 0, 0)
    grad_in, grad_out = lax.psum((term_in, term_out), ("rep", "dom"))
    return (logits, grad_in, grad_out)


def solution(mesh):
    placed = (
        P("rep", "dom", None, None, None, None),
        P("rep", "dom", None, None),
        P("rep", "dom", None, None),
        P("rep", "dom", None),
        P(("dom", "rep"), None),
        P(),
        P(),
        P(("dom", "rep"), None),
    )
    return jax.shard_map(
        per_device,
        mesh=mesh,
        in_specs=placed,
        out_specs=(P(("dom", "rep"), None), P(), P()),
        check_vma=False,
    )
```

time: 807 us -> 468 us (0.58)
  waiting for transfers between devices: 655 us -> 336 us
  starting transfers between devices: 43.7 us -> 27.5 us
  blocking collectives: 15 us -> 30.3 us
  matrix products: 39.3 us -> 27.2 us
    all_to_all x3, waiting for transfers between devices: 295 us -> 80.3 us  [route(): lax.all_to_all(values, 'dom', split_axis=0, concat_axis=0, tiled=True)]
    reduce_scatter x1 -> x0, waiting for transfers between devices: 37.1 us -> none  [per_device(): lax.psum_scatter(partial_sum.astype(jnp.bfloat16), 'rep', scatter_dimensi...]
    all_to_all x2 -> x0, waiting for transfers between devices: 35.2 us -> none  [the longest x1 30.5 us: per_device(): lax.all_to_all(tiles, 'dom', split_axis=0, concat_axis=0, tiled=True)]
    all_gather x1 -> x0, waiting for transfers between devices: 32.5 us -> none  [aggregate(): block = lax.all_gather(values, 'rep', axis=0, tiled=True)]
    all_to_all x2 -> x0, starting transfers between devices: 16.6 us -> none  [the longest x1 11.9 us: per_device(): lax.all_to_all(cols, 'dom', split_axis=0, concat_axis=0, tiled=True)]
    all_gather x1 -> x2, blocking collectives: 15 us -> 30.3 us  [fetch(): block = lax.all_gather(values, 'rep', axis=0, tiled=True)]
    convert_element_type x5 -> x0, local copies, waits for them, and re-layouts: 14.1 us -> none  [the longest x2 11.3 us: aggregate(): ready = route(prod.astype(jnp.bfloat16))]
    select_n x4, local copies, waits for them, and re-layouts: 0.39 us -> 14.3 us  [the longest x2 14.1 us: per_device(): jnp.where(here[:, :, :, None, None], tiles[None], jnp.zeros_like(tiles)[N...]
  transfers between devices with their start and end apart: 8 -> 4, of which waited for: 8 -> 3; matrix products, arithmetic and copies ran while one was open for 7% -> 4% of each run, Pallas kernels for 0% -> 0%
where the time goes in v1:
time: 468 us; the launch traced here: 467 us
  waiting for transfers between devices  336 us (72%)
  local copies, waits for them, and re-layouts  31.2 us (7%)
  blocking collectives  30.3 us (6%)
  starting transfers between devices  27.5 us (6%)
  matrix products  27.2 us (6%)
  between operations  14.2 us (3%)
    psum x1, waiting for transfers between devices, per_device(): grad_in, grad_out = lax.psum((term_in, term_out), ('rep', 'dom'))  256 us
    all_to_all x3, waiting for transfers between devices, route(): lax.all_to_all(values, 'dom', split_axis=0, concat_axis=0, tiled=True)  80.3 us
    all_gather x2, blocking collectives, fetch(): block = lax.all_gather(values, 'rep', axis=0, tiled=True)  30.3 us
    all_to_all x3, starting transfers between devices, route(): lax.all_to_all(values, 'dom', split_axis=0, concat_axis=0, tiled=True)  27.3 us
    dot_general x7, matrix products, dot(): lax.dot_general(a, b, (((ca,), (cb,)), ((), ())), preferred_element_type=...  27.2 us
    select_n x2, local copies, waits for them, and re-layouts, per_device(): jnp.where(here[:, :, :, None, None], tiles[None], jnp.zeros_like(tiles)[N...  14.1 us
    unnamed x18, local copies, waits for them, and re-layouts  9.7 us
  transfers between devices with their start and end apart: 4, of which 3 were waited for; matrix products, arithmetic and copies ran while one was open for 4% of the time, Pallas kernels for 0%

profile of v1, /device:TPU:1, one launch (start us, length us, event | category | flops | bytes accessed | tf_op | source)
XLA Modules:
  0.0 466.8 jit_solution(9044114859213335009)
XLA Ops:
  7.2 0.0 copy-start
  7.2 1.4 copy.28
  8.6 11.9 %all-to-all-start = ((s32[32,1,2]{2,1,0:T(1,128)}), s32[32,1,2]{2,1,0:T(1,128)S(1)}, u32[]{:S(2)}, u32[]{:S(2)}) async-start(s32[32,1,2]{2,1,0:T(1,128)} %copy.28), calls=%async_computation | async-start | bytes 32768 | tf_op jit(solution)/shard_map/all_to_all | solution.py:8
  20.5 14.6 %all_gather.6 = bf16[2048,128]{1,0:T(8,128)(2,1)S(1)} all-gather(bf16[256,128]{1,0:T(8,128)(2,1)} %param.12), channel_id=1, replica_groups=mesh['rep'=8,'dom'=32] {'rep'}, dimensions={0}, use_global_device_ids=true | all-gather | bytes 589824 | tf_op jit(solution)/shard_map/all_gather | solution.py:34
  35.1 0.0 all-to-all-done
  35.1 0.1 copy.29
  35.2 0.1 copy.30
  35.3 0.1 reshape.98
  35.4 0.0 copy-start.3
  35.4 2.2 gather_fusion
  37.6 0.0 copy-start.7
  37.6 0.0 copy-start.6
  37.6 9.8 %all-to-all-start.1 = ((bf16[32,2,128,128]{3,2,1,0:T(8,128)(2,1)}), bf16[32,2,128,128]{3,2,1,0:T(8,128)(2,1)}, u32[]{:S(2)}, u32[]{:S(2)}) async-start(bf16[32,2,128,128]{3,2,1,0:T(8,128)(2,1)} %bitcast.7), calls=%async_computation.1 | async-start | bytes 4194304 | tf_op jit(solution)/shard_map/all_to_all | solution.py:8
  47.4 0.0 copy-done.3
  47.4 1.4 copy.26
  48.7 0.0 copy-done.7
  48.8 0.0 copy-done.6
  48.8 0.3 broadcast_select_fusion
  49.1 6.3 %copy.27 = bf16[2,128,32,2,128]{4,3,2,1,0:T(2,128)(2,1)} copy(bf16[2,128,32,2,128]{4,2,3,1,0:T(8,128)(2,1)S(1)} %broadcast_select_fusion) | data formatting | bytes 8388608 | tf_op jit(solution)/shard_map/jit(_where)/select_n | solution.py:29
  55.4 7.8 %select_n.28 = bf16[256,8192]{1,0:T(8,128)(2,1)} reshape(bf16[2,128,32,2,128]{4,3,2,1,0:T(2,128)(2,1)} %copy.27) | data formatting | bytes 8388608 | tf_op jit(solution)/shard_map/jit(_where)/select_n | solution.py:29
  63.2 32.5 %all-to-all-done.1 = bf16[32,2,128,128]{3,2,1,0:T(8,128)(2,1)} async-done(((bf16[32,2,128,128]{3,2,1,0:T(8,128)(2,1)}), bf16[32,2,128,128]{3,2,1,0:T(8,128)(2,1)}, u32[]{:S(2)}, u32[]{:S(2)}) %all-to-all-start.1) | async-done | bytes 2097184 | tf_op jit(solution)/shard_map/all_to_all | solution.py:8
  95.8 4.1 convolution_convert_fusion.2
  99.9 15.7 %all_gather.7 = bf16[2048,128]{1,0:T(8,128)(2,1)S(1)} all-gather(bf16[256,128]{1,0:T(8,128)(2,1)S(1)} %convolution_convert_fusion.2), channel_id=1, replica_groups=mesh['rep'=8,'dom'=32] {'rep'}, dimensions={0}, use_global_device_ids=true | all-gather | bytes 589824 | tf_op jit(solution)/shard_map/all_gather | solution.py:34
  115.5 0.0 copy-start.4
  115.5 0.0 copy-start.5
  115.5 2.1 gather_fusion.1
  117.7 5.7 %all-to-all-start.2 = ((bf16[32,2,128,128]{3,2,1,0:T(8,128)(2,1)}), bf16[32,2,128,128]{3,2,1,0:T(8,128)(2,1)S(1)}, u32[]{:S(2)}, u32[]{:S(2)}) async-start(bf16[32,2,128,128]{3,2,1,0:T(8,128)(2,1)} %bitcast.34), calls=%async_computation.2 | async-start | bytes 4194304 | tf_op jit(solution)/shard_map/all_to_all | solution.py:8
  123.3 0.2 all-reduce.3.cloned.1.call-start
  123.6 0.0 copy-done
  123.6 0.0 copy-done.4
  123.6 0.3 convolution_convert_fusion
  123.9 47.8 %all-to-all-done.2 = bf16[32,2,128,128]{3,2,1,0:T(8,128)(2,1)S(1)} async-done(((bf16[32,2,128,128]{3,2,1,0:T(8,128)(2,1)}), bf16[32,2,128,128]{3,2,1,0:T(8,128)(2,1)S(1)}, u32[]{:S(2)}, u32[]{:S(2)}) %all-to-all-start.2) | async-done | bytes 2097184 | tf_op jit(solution)/shard_map/all_to_all | solution.py:8
  171.7 0.0 copy-done.5
  171.7 0.0 copy-start.2
  171.7 2.3 fusion.13
  174.1 0.0 copy-start.1
  174.1 5.7 %copy-done.1 = f32[8192,512]{1,0:T(8,128)} copy-done((f32[8192,512]{1,0:T(8,128)}, f32[8192,512]{1,0:T(8,128)S(1)}, u32[]{:S(2)}) %copy-start.1) | copy-done | bytes 16777240
  179.8 0.0 copy-done.2
  179.8 4.2 fusion.7
  184.0 14.0 %fusion.2 = f32[128,512]{1,0:T(8,128)} fusion(bf16[8192,128]{1,0:T(8,128)(2,1)S(1)} %bitcast.33, f32[8192,512]{1,0:T(8,128)} %copy-done.1, bf16[256,8192]{1,0:T(8,128)(2,1)} %select_n.28, bf16[256,512]{1,0:T(8,128)(2,1)S(1)} %convolution_convert_fusion), kind=kOutput, calls=%fused_computation.6 | convolution fusion | flops 3258974208 | bytes 23592960 | tf_op jit(solution)/shard_map/dot_general | solution.py:12
  198.0 1.3 fusion.14
  199.3 0.0 all-reduce.3.cloned.1.call-update
  199.3 1.0 convolution_convert_fusion.1
  200.3 255.7 %all-reduce.3.cloned.1.call-done = (f32[128,512]{1,0:T(8,128)}, f32[512,512]{1,0:T(8,128)}) async-done(((f32[128,512]{1,0:T(8,128)}, f32[512,512]{1,0:T(8,128)}), (f32[128,512]{1,0:T(8,128)}, f32[512,512]{1,0:T(8,128)})) %all-reduce.3.cloned.1.call-update) | async-done | bytes 1310736 | tf_op jit(solution)/shard_map/psum | solution.py:50
  456.0 1.7 copy.33
  457.7 2.3 copy.34
  (4 shorter events, 0.0 us)
Async XLA Ops:
  7.2 116.4 %copy-start = (bf16[512,512]{1,0:T(8,128)(2,1)S(1)}, bf16[512,512]{1,0:T(8,128)(2,1)}, u32[]{:S(2)}) copy-start(bf16[512,512]{1,0:T(8,128)(2,1)} %param.14) | copy-start | bytes 1572868
  8.6 26.5 %all-to-all-start = ((s32[32,1,2]{2,1,0:T(1,128)}), s32[32,1,2]{2,1,0:T(1,128)S(1)}, u32[]{:S(2)}, u32[]{:S(2)}) async-start(s32[32,1,2]{2,1,0:T(1,128)} %copy.28), calls=%async_computation | async-start | bytes 32768 | tf_op jit(solution)/shard_map/all_to_all | solution.py:8
  35.4 12.0 %copy-start.3 = (bf16[1,1,32,2,128,128]{5,4,3,2,1,0:T(8,128)(2,1)S(1)}, bf16[1,1,32,2,128,128]{5,4,3,2,1,0:T(8,128)(2,1)}, u32[]{:S(2)}) copy-start(bf16[1,1,32,2,128,128]{5,4,3,2,1,0:T(8,128)(2,1)} %param.8) | copy-start | bytes 6291460
  37.6 11.1 %copy-start.7 = (s32[1,1,32]{2,1,0:T(1,128)S(1)}, s32[1,1,32]{2,1,0:T(1,128)}, u32[]{:S(2)}) copy-start(s32[1,1,32]{2,1,0:T(1,128)} %param.11) | copy-start | bytes 388
  37.6 11.2 %copy-start.6 = (s32[1,1,32,2]{2,3,1,0:T(2,128)S(1)}, s32[1,1,32,2]{2,3,1,0:T(2,128)}, u32[]{:S(2)}) copy-start(s32[1,1,32,2]{2,3,1,0:T(2,128)} %param.9) | copy-start | bytes 772
  37.6 58.2 %all-to-all-start.1 = ((bf16[32,2,128,128]{3,2,1,0:T(8,128)(2,1)}), bf16[32,2,128,128]{3,2,1,0:T(8,128)(2,1)}, u32[]{:S(2)}, u32[]{:S(2)}) async-start(bf16[32,2,128,128]{3,2,1,0:T(8,128)(2,1)} %bitcast.7), calls=%async_computation.1 | async-start | bytes 4194304 | tf_op jit(solution)/shard_map/all_to_all | solution.py:8
  115.5 8.1 %copy-start.4 = (bf16[256,512]{1,0:T(8,128)(2,1)S(1)}, bf16[256,512]{1,0:T(8,128)(2,1)}, u32[]{:S(2)}) copy-start(bf16[256,512]{1,0:T(8,128)(2,1)} %param.15) | copy-start | bytes 786436
  115.5 56.2 %copy-start.5 = (bf16[128,512]{1,0:T(8,128)(2,1)S(1)}, bf16[128,512]{1,0:T(8,128)(2,1)}, u32[]{:S(2)}) copy-start(bf16[128,512]{1,0:T(8,128)(2,1)} %param.13) | copy-start | bytes 393220
  117.7 54.1 %all-to-all-start.2 = ((bf16[32,2,128,128]{3,2,1,0:T(8,128)(2,1)}), bf16[32,2,128,128]{3,2,1,0:T(8,128)(2,1)S(1)}, u32[]{:S(2)}, u32[]{:S(2)}) async-start(bf16[32,2,128,128]{3,2,1,0:T(8,128)(2,1)} %bitcast.34), calls=%async_computation.2 | async-start | bytes 4194304 | tf_op jit(solution)/shard_map/all_to_all | solution.py:8
  123.3 332.6 %all-reduce.3.cloned.1.call-start = ((), (), s32[]{:S(2)}) async-start(), calls=%async_computation.3 | async-start | bytes 2621440 | tf_op jit(solution)/shard_map/psum | solution.py:50
  171.7 8.1 %copy-start.2 = (bf16[256,8192]{1,0:T(8,128)(2,1)S(1)}, bf16[256,8192]{1,0:T(8,128)(2,1)}, u32[]{:S(2)}) copy-start(bf16[256,8192]{1,0:T(8,128)(2,1)} %select_n.28) | copy-start | bytes 12582916
  174.1 5.7 %copy-start.1 = (f32[8192,512]{1,0:T(8,128)}, f32[8192,512]{1,0:T(8,128)S(1)}, u32[]{:S(2)}) copy-start(f32[8192,512]{1,0:T(8,128)S(1)} %fusion.13) | copy-start | bytes 50331652
Sparse Core Ops, SparseCore 0:
  199.4 256.5 all-reduce.2

commit v2 on v1

v2 whole, which is shorter than its diff:
```python
import functools

import jax
import jax.numpy as jnp
from jax import lax
from jax.experimental import pallas as pl
from jax.experimental.pallas import tpu as pltpu
from jax.sharding import PartitionSpec as P

BF = jnp.bfloat16
F32 = jnp.float32

NY, NK, NZ, NX = 4, 2, 8, 4
NR = NY * NK
ND = NZ * NX
SLOTS = 2
TILE = 128
OWN = 2
BLOCKS = NR * OWN
HALF = BLOCKS // NK
STEPS = NZ // 2
GROUPS = NZ
PLANE = NY * NX
LANES = 640
CHUNK = 16
CHUNKS = 512 // CHUNK
SHARE = CHUNKS // NK

OFFSET = [0] + [s * t for t in range(1, STEPS) for s in (-1, 1)] + [STEPS]


def group_of(way, step):
    if step == 0:
        return 0
    if step == STEPS:
        return GROUPS - 1
    return 2 * step - 1 + way


def dot(a, b, ca, cb):
    return lax.dot_general(a, b, (((ca,), (cb,)), ((), ())), preferred_element_type=F32)


def kernel(*refs):
    refs = list(refs)

    def take(n):
        out, refs[:n] = refs[:n], []
        return out

    tiles, rows_s, cols_s, counts_s, cols_v, feat, w_in, w_out, cot = take(9)
    logits, grad_in, grad_out = take(3)
    raw = [take(GROUPS), take(GROUPS)]
    picked = take(2)
    sending = take(2)
    far_v, far_s, spread, w_in_t, dagg_t, acc1, agg1, acc2, acc3 = take(9)
    part, red1_out, red1_in, red2_out, red2_in, red3, full = take(7)
    a_s, a_r, b_s, b_r, p_s, p_r, c_s, c_r, col_s, col_r, loc = take(11)
    g1_s, g1_r, g2_s, g2_r, g3_s, g3_r, g4_s, g4_r, g5_s, g5_r = take(10)

    r = lax.axis_index("rep")
    d = lax.axis_index("dom")
    y, k = r // NK, r % NK
    z, x = d // NX, d % NX
    left = []

    def send(src, dst, s_sem, r_sem, rr, zz, xx):
        copy = pltpu.make_async_remote_copy(
            src_ref=src,
            dst_ref=dst,
            send_sem=s_sem,
            recv_sem=r_sem,
            device_id=(rr, zz * NX + xx),
            device_id_type=pl.DeviceIdType.MESH,
        )
        copy.start()
        left.append(copy)
        return copy

    greet = [((r + i) % NR, z, x) for i in range(1, NR)]
    for dx in range(1, NX):
        for dy in range(NY):
            greet.append((((y + dy) % NY) * NK + k, z, (x + dx) % NX))
    for dz in range(1, NZ):
        greet.append((r, (z + dz) % NZ, x))
    barrier = pltpu.get_barrier_semaphore()
    for rr, zz, xx in greet:
        pl.semaphore_signal(
            barrier, inc=1, device_id=(rr, zz * NX + xx), device_id_type=pl.DeviceIdType.MESH
        )
    pl.semaphore_wait(barrier, len(greet))

    def gather_rep(p, own):
        copies = []
        for i in range(1, NR):
            copies.append(
                send(
                    own,
                    raw[p][0].at[pl.ds(OWN * r, OWN)],
                    a_s.at[p, i - 1],
                    a_r.at[p, i - 1],
                    (r + i) % NR,
                    z,
                    x,
                )
            )
        raw[p][0][pl.ds(OWN * r, OWN)] = own[...]
        return copies

    def ring(p, way, step):
        if step < STEPS:
            where = pl.ds(HALF * k, HALF)
        else:
            where = pl.ds(HALF * k + way * (HALF // 2), HALF // 2)
        return send(
            raw[p][group_of(way, step - 1)].at[where],
            raw[p][group_of(way, step)].at[where],
            b_s.at[p, way, step - 1],
            b_r.at[p, way, step - 1],
            r,
            (z + (1, NZ - 1)[way]) % NZ,
            x,
        )

    def share(p, g):
        where = pl.ds(HALF * k, HALF)
        return send(
            raw[p][g].at[where],
            raw[p][g].at[where],
            p_s.at[p, g - 1],
            p_r.at[p, g - 1],
            y * NK + 1 - k,
            z,
            x,
        )

    def pick(p, g):
        c = ((z + OFFSET[g] + NZ) % NZ) * NX + x
        copies = []
        for dx in range(1, NX):
            for s in range(SLOTS):
                j = far_s[dx - 1, 0, c * SLOTS + s]
                sending[p][g, dx - 1, s] = raw[p][g][j]
            copies.append(
                send(
                    sending[p].at[g, dx - 1],
                    picked[p].at[g, x],
                    c_s.at[p, g, dx - 1],
                    c_r.at[p, g, dx - 1],
                    r,
                    z,
                    (x + dx) % NX,
                )
            )
        for s in range(SLOTS):
            picked[p][g, x, s] = raw[p][g][cols_s[c * SLOTS + s]]
        return copies

    def exchange(p, own, early, meanwhile, consume):
        copies = gather_rep(p, own)
        early()
        for copy in copies:
            copy.wait_recv()
        going = [ring(p, 0, 1), ring(p, 1, 1)]
        coming = [(0, pick(p, 0))]
        meanwhile()
        for step in range(1, STEPS + 1):
            shares = []
            later = []
            if step < STEPS:
                for way in (0, 1):
                    going[way].wait_recv()
                    later.append(ring(p, way, step + 1))
                    g = group_of(way, step)
                    shares.append((g, share(p, g)))
            else:
                going[0].wait_recv()
                going[1].wait_recv()
                shares.append((GROUPS - 1, share(p, GROUPS - 1)))
            going = later
            fresh = []
            for g, copy in shares:
                copy.wait_recv()
                fresh.append((g, pick(p, g)))
            for g, copies in coming:
                for copy in copies:
                    copy.wait_recv()
                consume(g)
            coming = fresh
        for g, copies in coming:
            for copy in copies:
                copy.wait_recv()
            consume(g)

    col_copies = [
        send(cols_v, far_v.at[dx - 1], col_s.at[dx - 1], col_r.at[dx - 1], r, z, (x + NX - dx) % NX)
        for dx in range(1, NX)
    ]

    def early1():
        for copy in col_copies:
            copy.wait_recv()
        local = pltpu.make_async_copy(far_v, far_s, loc.at[0])
        local.start()
        local.wait()

    def meanwhile1():
        for g in range(GROUPS):
            zc = (z + OFFSET[g] + NZ) % NZ

            def place(xc, carry, g=g, zc=zc):
                c = zc * NX + xc
                for s in range(SLOTS):
                    tile = tiles[c, s]
                    row = rows_s[c * SLOTS + s]
                    live = s < counts_s[c]
                    for b in range(OWN):
                        spread[g * NX + xc, b * TILE : (b + 1) * TILE, s * TILE : (s + 1) * TILE] = (
                            jnp.where(jnp.logical_and(live, row == b), tile, jnp.zeros_like(tile))
                        )
                return carry

            lax.fori_loop(0, NX, place, 0)
        w_in_t[...] = w_in[...].astype(F32).T.astype(BF)
        dagg_t[...] = dot(w_out[...], cot[...], 1, 1).astype(BF)
        acc1[...] = jnp.zeros_like(acc1)
        acc2[...] = jnp.zeros_like(acc2)
        acc3[...] = jnp.zeros_like(acc3)

    def consume1(g):
        def body(xc, carry):
            near = picked[0][g, xc].reshape(SLOTS * TILE, TILE)
            acc1[...] += dot(spread[g * NX + xc], near, 1, 0)
            return carry

        lax.fori_loop(0, NX, body, 0)

    exchange(0, feat, early1, meanwhile1, consume1)
    agg1[...] = acc1[...].astype(BF).reshape(OWN, TILE, TILE)

    def consume2(g):
        def body(xc, carry):
            near = picked[1][g, xc].reshape(SLOTS * TILE, TILE)
            tile = spread[g * NX + xc]
            z1 = dot(w_in_t[...], near, 1, 1)
            sig = 0.5 + 0.5 * jnp.tanh(0.5 * z1)
            hidden = z1 * sig
            slope = sig + hidden * (1.0 - sig)
            acc2[...] += dot(hidden.astype(BF), tile, 1, 1)
            dz = (dot(dagg_t[...], tile, 1, 0) * slope).astype(BF)
            acc3[...] += dot(dz, near, 1, 0)
            return carry

        lax.fori_loop(0, NX, body, 0)

    exchange(1, agg1, lambda: None, lambda: None, consume2)

    agg2_t = acc2[...].astype(BF)
    part[:, :, 0:512] = dot(agg2_t, cot[...], 1, 0).reshape(CHUNKS, CHUNK, 512)
    part[:, :, 512:LANES] = acc3[...].reshape(CHUNKS, CHUNK, TILE)

    mine = pl.ds(SHARE * k, SHARE)
    red1_out[...] = part[pl.ds(SHARE * (1 - k), SHARE)].astype(BF)
    copy = send(red1_out, red1_in, g1_s.at[0], g1_r.at[0], y * NK + 1 - k, z, x)
    logits[...] = dot(agg2_t, w_out[...], 0, 0).astype(BF)
    copy.wait_recv()
    red2_out[...] = (part[mine] + red1_in[...].astype(F32)).astype(BF)
    me = y * NX + x
    plane = [(dy, dx) for dy in range(NY) for dx in range(NX) if dy or dx]
    copies = []
    for i, (dy, dx) in enumerate(plane):
        yy, xx = (y + dy) % NY, (x + dx) % NX
        copies.append(
            send(red2_out.at[yy * NX + xx], red2_in.at[i], g2_s.at[i], g2_r.at[i], yy * NK + k, z, xx)
        )
    for copy in copies:
        copy.wait_recv()
    total = red2_out[me].astype(F32)
    for i in range(PLANE - 1):
        total = total + red2_in[i].astype(F32)
    red3[z] = total.astype(BF)
    copies = [
        send(red3.at[z], red3.at[z], g3_s.at[i - 1], g3_r.at[i - 1], r, (z + i) % NZ, x)
        for i in range(1, NZ)
    ]
    for copy in copies:
        copy.wait_recv()
    total = red3[0].astype(F32)
    for i in range(1, NZ):
        total = total + red3[i].astype(F32)
    full[SHARE * k + me] = total.astype(BF)
    copies = []
    for i, (dy, dx) in enumerate(plane):
        yy, xx = (y + dy) % NY, (x + dx) % NX
        at = full.at[SHARE * k + me]
        copies.append(send(at, at, g4_s.at[i], g4_r.at[i], yy * NK + k, z, xx))
    for copy in copies:
        copy.wait_recv()
    copy = send(full.at[mine], full.at[mine], g5_s.at[0], g5_r.at[0], y * NK + 1 - k, z, x)
    copy.wait_recv()
    grad_out[...] = full[:, :, 0:512].astype(F32).reshape(512, 512)
    grad_in[...] = full[:, :, 512:LANES].astype(F32).reshape(512, TILE).T
    for copy in left:
        copy.wait_send()


def per_device(
    tile_values, tile_rows, tile_cols, tile_counts, features, weight_in, weight_out, cotangent
):
    cols = tile_cols.reshape(ND * SLOTS)
    cols_v = jnp.pad(cols.reshape(1, ND * SLOTS), ((0, 7), (0, TILE - ND * SLOTS)))
    vmem = pl.BlockSpec(memory_space=pltpu.VMEM)
    smem = pl.BlockSpec(memory_space=pltpu.SMEM)
    block = pltpu.VMEM((BLOCKS, TILE, TILE), BF)
    dma = pltpu.SemaphoreType.DMA
    scratch = [block] * (2 * GROUPS)
    scratch += [pltpu.VMEM((GROUPS, NX, SLOTS, TILE, TILE), BF)] * 2
    scratch += [pltpu.VMEM((GROUPS, NX - 1, SLOTS, TILE, TILE), BF)] * 2
    scratch += [
        pltpu.VMEM((NX - 1, 8, TILE), jnp.int32),
        pltpu.SMEM((NX - 1, 8, TILE), jnp.int32),
        pltpu.VMEM((ND, 256, 256), BF),
        pltpu.VMEM((512, TILE), BF),
        pltpu.VMEM((512, 256), BF),
        pltpu.VMEM((256, TILE), F32),
        pltpu.VMEM((OWN, TILE, TILE), BF),
        pltpu.VMEM((512, 256), F32),
        pltpu.VMEM((512, TILE), F32),
        pltpu.VMEM((CHUNKS, CHUNK, LANES), F32),
        pltpu.VMEM((SHARE, CHUNK, LANES), BF),
        pltpu.VMEM((SHARE, CHUNK, LANES), BF),
        pltpu.VMEM((SHARE, CHUNK, LANES), BF),
        pltpu.VMEM((PLANE - 1, CHUNK, LANES), BF),
        pltpu.VMEM((NZ, CHUNK, LANES), BF),
        pltpu.VMEM((CHUNKS, CHUNK, LANES), BF),
    ]
    for shape in (
        (2, NR - 1),
        (2, 2, STEPS),
        (2, GROUPS - 1),
        (2, GROUPS, NX - 1),
        (NX - 1,),
    ):
        scratch += [dma(shape)] * 2
    scratch += [dma((1,))]
    for count in (1, PLANE - 1, NZ - 1, PLANE - 1, 1):
        scratch += [dma((count,))] * 2
    logits, grad_in, grad_out = pl.pallas_call(
        kernel,
        out_shape=(
            jax.ShapeDtypeStruct((256, 512), BF),
            jax.ShapeDtypeStruct((TILE, 512), F32),
            jax.ShapeDtypeStruct((512, 512), F32),
        ),
        in_specs=[vmem, smem, smem, smem] + [vmem] * 5,
        out_specs=(vmem,) * 3,
        scratch_shapes=scratch,
        compiler_params=pltpu.CompilerParams(
            collective_id=0, has_side_effects=True, vmem_limit_bytes=48 * 1024 * 1024
        ),
        cost_estimate=pl.CostEstimate(
            flops=5_000_000_000, bytes_accessed=5_000_000, transcendentals=4_000_000
        ),
    )(
        tile_values.reshape(ND, SLOTS, TILE, TILE),
        tile_rows.reshape(ND * SLOTS),
        cols,
        tile_counts.reshape(ND),
        cols_v,
        features.reshape(OWN, TILE, TILE),
        weight_in,
        weight_out,
        cotangent,
    )
    return logits, grad_in, grad_out


def solution(mesh):
    placed = (
        P("rep", "dom", None, None, None, None),
        P("rep", "dom", None, None),
        P("rep", "dom", None, None),
        P("rep", "dom", None),
        P(("dom", "rep"), None),
        P(),
        P(),
        P(("dom", "rep"), None),
    )
    return jax.shard_map(
        per_device,
        mesh=mesh,
        in_specs=placed,
        out_specs=(P(("dom", "rep"), None), P(), P()),
        check_vma=False,
    )
```

time: 468 us -> 136 us (0.29)
  waiting for transfers between devices: 336 us -> 0 us
  Pallas kernels: 0 us -> 125 us
  blocking collectives: 30.3 us -> 0 us
  starting transfers between devices: 27.5 us -> 0 us
  matrix products: 27.2 us -> 0 us
  local copies, waits for them, and re-layouts: 31.2 us -> 10.2 us
  between operations: 14.2 us -> 0.67 us
    psum x1 -> x0, waiting for transfers between devices: 256 us -> none  [per_device(): grad_in, grad_out = lax.psum((term_in, term_out), ('rep', 'dom'))]
    pallas_call x0 -> x1, Pallas kernels: none -> 125 us  [per_device(): pl.pallas_call(kernel, out_shape=(jax.ShapeDtypeStruct((256, 512), BF), j...]
    all_to_all x3 -> x0, waiting for transfers between devices: 80.3 us -> none  [route(): lax.all_to_all(values, 'dom', split_axis=0, concat_axis=0, tiled=True)]
    all_gather x2 -> x0, blocking collectives: 30.3 us -> none  [fetch(): block = lax.all_gather(values, 'rep', axis=0, tiled=True)]
    all_to_all x3 -> x0, starting transfers between devices: 27.3 us -> none  [route(): lax.all_to_all(values, 'dom', split_axis=0, concat_axis=0, tiled=True)]
    dot_general x7 -> x0, matrix products: 27.2 us -> none  [dot(): lax.dot_general(a, b, (((ca,), (cb,)), ((), ())), preferred_element_type=...]
    select_n x4 -> x0, local copies, waits for them, and re-layouts: 14.3 us -> none  [the longest x2 14.1 us: per_device(): jnp.where(here[:, :, :, None, None], tiles[None], jnp.zeros_like(tiles)[N...]
    unnamed x18 -> x17, local copies, waits for them, and re-layouts: 9.7 us -> 9.88 us
  transfers between devices with their start and end apart: 4 -> 0, of which waited for: 3 -> 0; matrix products, arithmetic and copies ran while one was open for 4% -> 0% of each run, Pallas kernels for 0% -> 0%
where the time goes in v2:
time: 136 us
  Pallas kernels  125 us (92%)
  local copies, waits for them, and re-layouts  10.2 us (7%)
    pallas_call x1, Pallas kernels, per_device(): pl.pallas_call(kernel, out_shape=(jax.ShapeDtypeStruct((256, 512), BF), j...  125 us
    unnamed x17, local copies, waits for them, and re-layouts  9.88 us

profile of v2, /device:TPU:1, one launch (start us, length us, event | category | flops | bytes accessed | tf_op | source)
XLA Modules:
  0.0 135.8 jit_solution(50932596133252909)
XLA Ops:
  0.6 0.8 copy.15
  1.4 0.1 reshape_reshape.3
  1.5 0.1 reshape.23.refs_2_
  1.6 0.8 copy.14
  2.4 0.1 reshape.22.refs_1_
  2.5 0.0 copy-start
  2.5 1.6 %copy-done = bf16[1,1,32,2,128,128]{5,4,3,2,1,0:T(8,128)(2,1)S(1)} copy-done((bf16[1,1,32,2,128,128]{5,4,3,2,1,0:T(8,128)(2,1)S(1)}, bf16[1,1,32,2,128,128]{5,4,3,2,1,0:T(8,128)(2,1)}, u32[]{:S(2)}) %copy-start) | copy-done | bytes 2097176
  4.1 0.0 copy-start.1
  4.1 1.0 copy-done.1
  5.1 0.0 copy-start.2
  5.1 0.9 copy-done.2
  6.1 0.0 copy-start.3
  6.1 0.9 copy-done.3
  7.0 0.0 copy-start.4
  7.0 0.8 copy-done.4
  7.8 0.0 copy-start.5
  7.8 0.7 copy-done.5
  8.5 124.9 %shard_map.103 = (bf16[256,512]{1,0:T(8,128)(2,1)S(1)}, f32[128,512]{1,0:T(8,128)S(1)}, f32[512,512]{1,0:T(8,128)S(1)}) custom-call(bf16[32,2,128,128]{3,2,1,0:T(8,128)(2,1)S(1)} %bitcast.9, s32[64]{0:T(128)S(1)} %reshape.22.refs_1_, s32[64]{0:T(128)S(1)} %reshape.23.refs_2_, s32[32]{0:T(128)S(1)} %bitcast.11, s32[8,128]{1,0:T(8,128)S(1)} %pad.4.refs_4_, ...), custom_call_target="tpu_custom_call" | custom-call | flops 5000000000 | bytes 5000000 | tf_op jit(solution)/shard_map/pallas_call | solution.py:348
  133.4 0.7 copy.20
  134.1 0.7 copy.21
  134.8 1.0 copy.22
  (1 shorter events, 0.0 us)
Async XLA Ops:
  2.5 1.6 %copy-start = (bf16[1,1,32,2,128,128]{5,4,3,2,1,0:T(8,128)(2,1)S(1)}, bf16[1,1,32,2,128,128]{5,4,3,2,1,0:T(8,128)(2,1)}, u32[]{:S(2)}) copy-start(bf16[1,1,32,2,128,128]{5,4,3,2,1,0:T(8,128)(2,1)} %param.8) | copy-start | bytes 6291460
  4.1 1.0 copy-start.1
  5.1 0.9 copy-start.2
  6.1 0.9 copy-start.3
  7.0 0.8 copy-start.4
  7.8 0.7 copy-start.5

commit v3 on v2

v3 whole, which is shorter than its diff:
```python
import jax
import jax.numpy as jnp
from jax import lax
from jax.experimental import pallas as pl
from jax.experimental.pallas import tpu as pltpu
from jax.sharding import PartitionSpec as P

BF = jnp.bfloat16
F32 = jnp.float32

NY, NK, NZ, NX = 4, 2, 8, 4
NR = NY * NK
ND = NZ * NX
SLOTS = 2
TILE = 128
OWN = 2
BLOCKS = NR * OWN
HALF = BLOCKS // NK
STEPS = NZ // 2
GROUPS = NZ
PLANE = NY * NX
LANES = 640
CHUNK = 16
CHUNKS = 512 // CHUNK
SHARE = CHUNKS // NK

OFFSET = [0] + [s * t for t in range(1, STEPS) for s in (-1, 1)] + [STEPS]


def group_of(way, step):
    if step == 0:
        return 0
    if step == STEPS:
        return GROUPS - 1
    return 2 * step - 1 + way


def dot(a, b, ca, cb):
    return lax.dot_general(a, b, (((ca,), (cb,)), ((), ())), preferred_element_type=F32)


def kernel(*refs):
    refs = list(refs)

    def take(n):
        out, refs[:n] = refs[:n], []
        return out

    tiles_h, rows_h, cols_h, counts_h, feat, w_in_h, w_out_h, cot_h = take(8)
    logits_h, full_h = take(2)
    raw = [take(GROUPS), take(GROUPS)]
    picked = take(2)
    sending = take(2)
    tiles, w_in, w_out, cot, rows_s, cols_s, counts_s = take(7)
    far_v, far_s, spread, w_in_t, dagg_t, acc1, agg1, acc2, acc3 = take(9)
    agg2_t, logits, red1_out, red1_in, red2_out, red2_in, red3, full = take(8)
    y_s, y_r, b_s, b_r, p_s, p_r, c_s, c_r, col_s, col_r, loc = take(11)
    g1_s, g1_r, g2_s, g2_r, g3_s, g3_r, g4_s, g4_r, g5_s, g5_r = take(10)

    r = lax.axis_index("rep")
    d = lax.axis_index("dom")
    y, k = r // NK, r % NK
    z, x = d // NX, d % NX
    left = []

    def send(src, dst, s_sem, r_sem, rr, zz, xx):
        copy = pltpu.make_async_remote_copy(
            src_ref=src,
            dst_ref=dst,
            send_sem=s_sem,
            recv_sem=r_sem,
            device_id=(rr, zz * NX + xx),
            device_id_type=pl.DeviceIdType.MESH,
        )
        copy.start()
        left.append(copy)
        return copy

    def fetch(i, src, dst):
        copy = pltpu.make_async_copy(src, dst, loc.at[i])
        copy.start()
        return copy

    small = [fetch(0, cols_h, cols_s), fetch(1, rows_h, rows_s), fetch(2, counts_h, counts_s)]
    large = [
        fetch(3, tiles_h, tiles),
        fetch(4, w_in_h, w_in),
        fetch(5, w_out_h, w_out),
        fetch(6, cot_h, cot),
    ]

    greet = [(y * NK + 1 - k, z, x)]
    for dx in range(NX):
        for dy in range(NY):
            if dx or dy:
                greet.append((((y + dy) % NY) * NK + k, z, (x + dx) % NX))
    for dz in range(1, NZ):
        greet.append((r, (z + dz) % NZ, x))
    barrier = pltpu.get_barrier_semaphore()
    for rr, zz, xx in greet:
        pl.semaphore_signal(
            barrier, inc=1, device_id=(rr, zz * NX + xx), device_id_type=pl.DeviceIdType.MESH
        )
    pl.semaphore_wait(barrier, len(greet))

    half = pl.ds(HALF * k, HALF)
    at = HALF * k + OWN * y

    def ring(p, own, way, step):
        first, count = (0, OWN) if step < STEPS else (way, 1)
        here = pl.ds(at + first, count)
        src = own if step == 1 else raw[p][group_of(way, step - 1)].at[here]
        return send(
            src,
            raw[p][group_of(way, step)].at[here],
            b_s.at[p, way, step - 1],
            b_r.at[p, way, step - 1],
            r,
            (z + (1, NZ - 1)[way]) % NZ,
            x,
        )

    def gather_y(p, own, g):
        here = pl.ds(at, OWN)
        return [
            send(
                own if g == 0 else raw[p][g].at[here],
                raw[p][g].at[here],
                y_s.at[p, g, dy - 1],
                y_r.at[p, g, dy - 1],
                ((y + dy) % NY) * NK + k,
                z,
                x,
            )
            for dy in range(1, NY)
        ]

    def relay(p, way, i):
        here = pl.ds(HALF * k + OWN * ((y + NY - i) % NY), OWN)
        g = group_of(way, 2)
        return send(
            raw[p][group_of(way, 1)].at[here],
            raw[p][g].at[here],
            y_s.at[p, g, i - 1],
            y_r.at[p, g, i - 1],
            r,
            (z + (1, NZ - 1)[way]) % NZ,
            x,
        )

    def share(p, g):
        return send(
            raw[p][g].at[half],
            raw[p][g].at[half],
            p_s.at[p, g],
            p_r.at[p, g],
            y * NK + 1 - k,
            z,
            x,
        )

    def block(p, g, j):
        return raw[p][g][((j >> 1) & 1) * HALF + (j >> 2) * OWN + (j & 1)]

    def pick(p, g):
        c = ((z + OFFSET[g] + NZ) % NZ) * NX + x
        copies = []
        for dx in (2, 1, 3):
            for s in range(SLOTS):
                sending[p][g, dx - 1, s] = block(p, g, far_s[dx - 1, s, c])
            copies.append(
                send(
                    sending[p].at[g, dx - 1],
                    picked[p].at[g, x],
                    c_s.at[p, g, dx - 1],
                    c_r.at[p, g, dx - 1],
                    r,
                    z,
                    (x + dx) % NX,
                )
            )
        for s in range(SLOTS):
            picked[p][g, x, s] = block(p, g, cols_s[s, c])
        return copies

    def exchange(p, own, keep, ready, early, meanwhile, consume):
        rings = {0: [ring(p, own, 0, 1), ring(p, own, 1, 1)]}
        ys = {0: gather_y(p, own, 0)}
        shares, picks = {}, {}
        keep()

        def do_z(step):
            for copy in rings[step - 1]:
                copy.wait_recv()
            if step < STEPS:
                rings[step] = [ring(p, own, 0, step + 1), ring(p, own, 1, step + 1)]
            for g in sorted({group_of(0, step), group_of(1, step)}):
                if step != 2:
                    ys[g] = gather_y(p, own, g)

        def do_y(g):
            for i, copy in enumerate(ys[g]):
                copy.wait_recv()
                if g in (1, 2):
                    ys.setdefault(g + 2, []).append(relay(p, g - 1, i + 1))
            if g == 0:
                ready()
            shares[g] = share(p, g)

        def do_k(g):
            shares[g].wait_recv()
            picks[g] = pick(p, g)

        def do_c(g):
            for copy in picks[g]:
                copy.wait_recv()

            def body(xc, carry):
                consume(g, xc)
                return carry

            lax.fori_loop(0, NX, body, 0)

        def do_last(g):
            consume(g, x)
            for dx, i in ((1, 1), (3, 2), (2, 0)):
                picks[g][i].wait_recv()
                consume(g, (x + NX - dx) % NX)

        meanwhile()
        do_z(1)
        do_y(0)
        early()
        do_k(0)
        do_z(2)
        do_y(1)
        do_k(1)
        do_z(3)
        do_y(2)
        do_k(2)
        do_c(0)
        do_y(3)
        do_z(4)
        do_k(3)
        do_c(1)
        do_y(5)
        do_k(5)
        do_c(2)
        do_y(4)
        do_k(4)
        do_c(3)
        do_y(6)
        do_k(6)
        do_c(5)
        do_y(7)
        do_k(7)
        do_c(4)
        do_c(6)
        do_last(7)

    col_copies = [
        send(cols_h, far_v.at[dx - 1], col_s.at[dx - 1], col_r.at[dx - 1], r, z, (x + NX - dx) % NX)
        for dx in range(1, NX)
    ]

    def early1():
        for copy in col_copies:
            copy.wait_recv()
        fetch(7, far_v, far_s).wait()

    kept = []

    def keep1():
        kept.append(fetch(8, feat, raw[0][0].at[pl.ds(at, OWN)]))

    def ready1():
        kept[0].wait()

    def keep2():
        raw[1][0][pl.ds(at, OWN)] = agg1[...]

    def meanwhile1():
        for copy in small + large:
            copy.wait()
        for g in range(GROUPS):
            zc = (z + OFFSET[g] + NZ) % NZ

            def place(xc, carry, g=g, zc=zc):
                c = zc * NX + xc
                for s in range(SLOTS):
                    tile = tiles[c, s]
                    row = rows_s[s, c]
                    live = s < counts_s[c]
                    for b in range(OWN):
                        spread[g * NX + xc, b * TILE : (b + 1) * TILE, s * TILE : (s + 1) * TILE] = (
                            jnp.where(jnp.logical_and(live, row == b), tile, jnp.zeros_like(tile))
                        )
                return carry

            lax.fori_loop(0, NX, place, 0)
        w_in_t[...] = w_in[...].astype(F32).T.astype(BF)
        dagg_t[...] = dot(w_out[...], cot[...], 1, 1).astype(BF)
        acc1[...] = jnp.zeros_like(acc1)
        acc2[...] = jnp.zeros_like(acc2)
        acc3[...] = jnp.zeros_like(acc3)

    def consume1(g, xc):
        near = picked[0][g, xc].reshape(SLOTS * TILE, TILE)
        acc1[...] += dot(spread[g * NX + xc], near, 1, 0)

    exchange(0, feat, keep1, ready1, early1, meanwhile1, consume1)
    agg1[...] = acc1[...].astype(BF).reshape(OWN, TILE, TILE)

    def consume2(g, xc):
        near = picked[1][g, xc].reshape(SLOTS * TILE, TILE)
        tile = spread[g * NX + xc]
        z1 = dot(w_in_t[...], near, 1, 1)
        sig = 0.5 + 0.5 * jnp.tanh(0.5 * z1)
        hidden = z1 * sig
        slope = sig + hidden * (1.0 - sig)
        acc2[...] += dot(hidden.astype(BF), tile, 1, 1)
        dz = (dot(dagg_t[...], tile, 1, 0) * slope).astype(BF)
        acc3[...] += dot(dz, near, 1, 0)

    def nothing():
        pass

    exchange(1, agg1, keep2, nothing, nothing, nothing, consume2)

    agg2_t[...] = acc2[...].astype(BF)

    def term(core):
        rows = pl.ds(256 * core, 256)
        return (
            dot(agg2_t[rows], cot[...], 1, 0).reshape(SHARE, CHUNK, 512),
            acc3[rows].reshape(SHARE, CHUNK, TILE),
        )

    out, back = term(1 - k)
    red1_out[:, :, 0:512] = out.astype(BF)
    red1_out[:, :, 512:LANES] = back.astype(BF)
    copy = send(red1_out, red1_in, g1_s.at[0], g1_r.at[0], y * NK + 1 - k, z, x)
    out, back = term(k)
    copy.wait_recv()
    red2_out[:, :, 0:512] = (out + red1_in[:, :, 0:512].astype(F32)).astype(BF)
    red2_out[:, :, 512:LANES] = (back + red1_in[:, :, 512:LANES].astype(F32)).astype(BF)
    me = y * NX + x
    plane = [(dy, dx) for dy in range(NY) for dx in range(NX) if dy or dx]
    plane.sort(key=lambda step: -min(step[0], NY - step[0]) - min(step[1], NX - step[1]))
    copies = []
    for i, (dy, dx) in enumerate(plane):
        yy, xx = (y + dy) % NY, (x + dx) % NX
        copies.append(
            send(red2_out.at[yy * NX + xx], red2_in.at[i], g2_s.at[i], g2_r.at[i], yy * NK + k, z, xx)
        )
    logits[...] = dot(agg2_t[...], w_out[...], 0, 0).astype(BF)
    done = fetch(0, logits, logits_h)
    total = red2_out[me].astype(F32)
    for i in range(PLANE - 2, -1, -1):
        copies[i].wait_recv()
        total = total + red2_in[i].astype(F32)
    red3[z] = total.astype(BF)
    copies = [
        send(red3.at[z], red3.at[z], g3_s.at[i - 1], g3_r.at[i - 1], r, (z + i) % NZ, x)
        for i in (4, 3, 5, 2, 6, 1, 7)
    ]
    for copy in copies:
        copy.wait_recv()
    total = red3[0].astype(F32)
    for i in range(1, NZ):
        total = total + red3[i].astype(F32)

    def to_core(i, chunk):
        return send(chunk, chunk, g5_s.at[i], g5_r.at[i], y * NK + 1 - k, z, x)

    full[SHARE * k + me] = total.astype(BF)
    chunk = full.at[SHARE * k + me]
    copies = []
    for i, (dy, dx) in enumerate(plane):
        yy, xx = (y + dy) % NY, (x + dx) % NX
        copies.append(send(chunk, chunk, g4_s.at[i], g4_r.at[i], yy * NK + k, z, xx))
    others = [to_core(PLANE - 1, chunk)]
    for i in range(PLANE - 2, -1, -1):
        copies[i].wait_recv()
        dy, dx = plane[i]
        came = ((y + NY - dy) % NY) * NX + (x + NX - dx) % NX
        others.append(to_core(i, full.at[SHARE * k + came]))
    for copy in others:
        copy.wait_recv()
    last = fetch(1, full, full_h)
    for copy in left:
        copy.wait_send()
    done.wait()
    last.wait()


def unpack(logits_in, full, logits, grad_in, grad_out):
    logits[...] = logits_in[...]
    grad_out[...] = full[:, :, 0:512].astype(F32).reshape(512, 512)
    grad_in[...] = full[:, :, 512:LANES].astype(F32).reshape(512, TILE).T


def per_device(
    tile_values, tile_rows, tile_cols, tile_counts, features, weight_in, weight_out, cotangent
):
    vmem = pl.BlockSpec(memory_space=pltpu.VMEM)
    hbm = pl.BlockSpec(memory_space=pltpu.HBM)
    block = pltpu.VMEM((BLOCKS, TILE, TILE), BF)
    dma = pltpu.SemaphoreType.DMA
    scratch = [block] * (2 * GROUPS)
    scratch += [pltpu.VMEM((GROUPS, NX, SLOTS, TILE, TILE), BF)] * 2
    scratch += [pltpu.VMEM((GROUPS, NX - 1, SLOTS, TILE, TILE), BF)] * 2
    scratch += [
        pltpu.VMEM((ND, SLOTS, TILE, TILE), BF),
        pltpu.VMEM((TILE, 512), BF),
        pltpu.VMEM((512, 512), BF),
        pltpu.VMEM((256, 512), BF),
        pltpu.SMEM((SLOTS, ND), jnp.int32),
        pltpu.SMEM((SLOTS, ND), jnp.int32),
        pltpu.SMEM((ND,), jnp.int32),
        pltpu.VMEM((NX - 1, SLOTS, ND), jnp.int32),
        pltpu.SMEM((NX - 1, SLOTS, ND), jnp.int32),
        pltpu.VMEM((ND, 256, 256), BF),
        pltpu.VMEM((512, TILE), BF),
        pltpu.VMEM((512, 256), BF),
        pltpu.VMEM((256, TILE), F32),
        pltpu.VMEM((OWN, TILE, TILE), BF),
        pltpu.VMEM((512, 256), F32),
        pltpu.VMEM((512, TILE), F32),
        pltpu.VMEM((512, 256), BF),
        pltpu.VMEM((256, 512), BF),
        pltpu.VMEM((SHARE, CHUNK, LANES), BF),
        pltpu.VMEM((SHARE, CHUNK, LANES), BF),
        pltpu.VMEM((SHARE, CHUNK, LANES), BF),
        pltpu.VMEM((PLANE - 1, CHUNK, LANES), BF),
        pltpu.VMEM((NZ, CHUNK, LANES), BF),
        pltpu.VMEM((CHUNKS, CHUNK, LANES), BF),
    ]
    for shape in (
        (2, GROUPS, NY - 1),
        (2, 2, STEPS),
        (2, GROUPS),
        (2, GROUPS, NX - 1),
        (NX - 1,),
    ):
        scratch += [dma(shape)] * 2
    scratch += [dma((9,))]
    for count in (1, PLANE - 1, NZ - 1, PLANE - 1, PLANE):
        scratch += [dma((count,))] * 2
    logits, full = pl.pallas_call(
        kernel,
        out_shape=(
            jax.ShapeDtypeStruct((256, 512), BF),
            jax.ShapeDtypeStruct((CHUNKS, CHUNK, LANES), BF),
        ),
        in_specs=[hbm] * 8,
        out_specs=(hbm,) * 2,
        scratch_shapes=scratch,
        compiler_params=pltpu.CompilerParams(
            collective_id=0, has_side_effects=True, vmem_limit_bytes=60 * 1024 * 1024
        ),
        cost_estimate=pl.CostEstimate(
            flops=5_000_000_000, bytes_accessed=5_000_000, transcendentals=4_000_000
        ),
    )(
        tile_values.reshape(ND, SLOTS, TILE, TILE),
        tile_rows[0, 0].T,
        tile_cols[0, 0].T,
        tile_counts.reshape(ND),
        features.reshape(OWN, TILE, TILE),
        weight_in,
        weight_out,
        cotangent,
    )
    return pl.pallas_call(
        unpack,
        out_shape=(
            jax.ShapeDtypeStruct((256, 512), BF),
            jax.ShapeDtypeStruct((TILE, 512), F32),
            jax.ShapeDtypeStruct((512, 512), F32),
        ),
        in_specs=[vmem, vmem],
        out_specs=(vmem, vmem, vmem),
        compiler_params=pltpu.CompilerParams(vmem_limit_bytes=60 * 1024 * 1024),
    )(logits, full)


def solution(mesh):
    placed = (
        P("rep", "dom", None, None, None, None),
        P("rep", "dom", None, None),
        P("rep", "dom", None, None),
        P("rep", "dom", None),
        P(("dom", "rep"), None),
        P(),
        P(),
        P(("dom", "rep"), None),
    )
    return jax.shard_map(
        per_device,
        mesh=mesh,
        in_specs=placed,
        out_specs=(P(("dom", "rep"), None), P(), P()),
        check_vma=False,
    )
```

time: 136 us -> 111 us (0.82)
  Pallas kernels: 125 us -> 110 us
  local copies, waits for them, and re-layouts: 10.2 us -> 0 us
    pallas_call x1, Pallas kernels: 125 us -> 108 us  [per_device(): pl.pallas_call(kernel, out_shape=(jax.ShapeDtypeStruct((256, 512), BF), j...]
    unnamed x17 -> x0, local copies, waits for them, and re-layouts: 9.88 us -> none
    pallas_call x0 -> x1, Pallas kernels: none -> 2.35 us  [per_device(): pl.pallas_call(unpack, out_shape=(jax.ShapeDtypeStruct((256, 512), BF), j...]
where the time goes in v3:
time: 111 us
  Pallas kernels  110 us (99%)
    pallas_call x1, Pallas kernels, per_device(): pl.pallas_call(kernel, out_shape=(jax.ShapeDtypeStruct((256, 512), BF), j...  108 us
    pallas_call x1, Pallas kernels, per_device(): pl.pallas_call(unpack, out_shape=(jax.ShapeDtypeStruct((256, 512), BF), j...  2.35 us

profile of v3, /device:TPU:1, one launch (start us, length us, event | category | flops | bytes accessed | tf_op | source)
XLA Modules:
  0.0 111.1 jit_solution(10243933450631708094)
XLA Ops:
  0.6 108.1 %shard_map.103 = (bf16[256,512]{1,0:T(8,128)(2,1)}, bf16[32,16,640]{2,1,0:T(8,128)(2,1)}) custom-call(bf16[32,2,128,128]{3,2,1,0:T(8,128)(2,1)} %bitcast.9, s32[2,32]{1,0:T(2,128)} %bitcast.11, s32[2,32]{1,0:T(2,128)} %bitcast.12, s32[32]{0:T(128)} %bitcast.13, bf16[2,128,128]{2,1,0:T(8,128)(2,1)} %bitcast.10, bf16[128,512]{1,0:T(8,128)(2,1)} %refs_5_.1, ...), custom_call_target="tpu_custom_call" | custom-call | flops 5000000000 | bytes 5000000 | tf_op jit(solution)/shard_map/pallas_call | solution.py:450
  108.7 2.4 %shard_map.104 = (bf16[256,512]{1,0:T(8,128)(2,1)}, f32[128,512]{1,0:T(8,128)}, f32[512,512]{1,0:T(8,128)}) custom-call(bf16[256,512]{1,0:T(8,128)(2,1)} %get-tuple-element.5.logits_in, bf16[32,16,640]{2,1,0:T(8,128)(2,1)} %get-tuple-element.6.full), custom_call_target="tpu_custom_call" | custom-call | tf_op jit(solution)/shard_map/pallas_call | solution.py:475

commit v4 on v3

--- a/solution.py
+++ b/solution.py
@@ -16,6 +16,7 @@
 OWN = 2
 BLOCKS = NR * OWN
 HALF = BLOCKS // NK
+MOVED = (6, 7)
 STEPS = NZ // 2
 GROUPS = NZ
 PLANE = NY * NX
@@ -52,9 +53,12 @@
     picked = take(2)
     sending = take(2)
     tiles, w_in, w_out, cot, rows_s, cols_s, counts_s = take(7)
+    far_rows_v, far_rows_s, far_counts_v, far_counts_s = take(4)
+    far_tiles, far_spread, far_near, far_acc, far_out, far_in = take(6)
     far_v, far_s, spread, w_in_t, dagg_t, acc1, agg1, acc2, acc3 = take(9)
     agg2_t, logits, red1_out, red1_in, red2_out, red2_in, red3, full = take(8)
     y_s, y_r, b_s, b_r, p_s, p_r, c_s, c_r, col_s, col_r, loc = take(11)
+    t_s, t_r, row_s, row_r, count_s, count_r, f_s, f_r = take(8)
     g1_s, g1_r, g2_s, g2_r, g3_s, g3_r, g4_s, g4_r, g5_s, g5_r = take(10)
 
     r = lax.axis_index("rep")
@@ -183,7 +187,7 @@
             picked[p][g, x, s] = block(p, g, cols_s[s, c])
         return copies
 
-    def exchange(p, own, keep, ready, early, meanwhile, consume):
+    def exchange(p, own, keep, ready, early, meanwhile, middle, consume):
         rings = {0: [ring(p, own, 0, 1), ring(p, own, 1, 1)]}
         ys = {0: gather_y(p, own, 0)}
         shares, picks = {}, {}
@@ -214,63 +218,103 @@
         def do_c(g):
             for copy in picks[g]:
                 copy.wait_recv()
-
-            def body(xc, carry):
-                consume(g, xc)
-                return carry
-
-            lax.fori_loop(0, NX, body, 0)
+            consume(g, range(NX))
 
         def do_last(g):
-            consume(g, x)
-            for dx, i in ((1, 1), (3, 2), (2, 0)):
-                picks[g][i].wait_recv()
-                consume(g, (x + NX - dx) % NX)
+            consume(g, [x])
+            picks[g][1].wait_recv()
+            picks[g][2].wait_recv()
+            consume(g, [(x + 1) % NX, (x + NX - 1) % NX])
+            picks[g][0].wait_recv()
+            consume(g, [(x + 2) % NX])
+
+        def do_w(g):
+            if p == 0 and g in MOVED:
+                shares[g].wait_recv()
+                moved(g)
+            else:
+                do_k(g)
 
         meanwhile()
         do_z(1)
+        early()
         do_y(0)
-        early()
-        do_k(0)
+        do_w(0)
         do_z(2)
         do_y(1)
-        do_k(1)
+        do_w(1)
         do_z(3)
         do_y(2)
-        do_k(2)
-        do_c(0)
+        do_w(2)
+        middle()
         do_y(3)
         do_z(4)
-        do_k(3)
+        do_w(3)
+        do_c(0)
+        do_y(5)
+        do_w(5)
+        do_y(4)
+        do_w(4)
         do_c(1)
-        do_y(5)
-        do_k(5)
+        do_y(6)
+        do_w(6)
         do_c(2)
-        do_y(4)
-        do_k(4)
+        do_y(7)
+        do_w(7)
         do_c(3)
-        do_y(6)
-        do_k(6)
         do_c(5)
-        do_y(7)
-        do_k(7)
         do_c(4)
-        do_c(6)
-        do_last(7)
-
-    col_copies = [
-        send(cols_h, far_v.at[dx - 1], col_s.at[dx - 1], col_r.at[dx - 1], r, z, (x + NX - dx) % NX)
-        for dx in range(1, NX)
-    ]
+        if p == 1:
+            do_c(6)
+            do_last(7)
+
+    tables = []
+    for dx in range(1, NX):
+        to = (r, z, (x + NX - dx) % NX)
+        i = dx - 1
+        tables.append(send(cols_h, far_v.at[i], col_s.at[i], col_r.at[i], *to))
+        tables.append(send(rows_h, far_rows_v.at[i], row_s.at[i], row_r.at[i], *to))
+        tables.append(send(counts_h, far_counts_v.at[i], count_s.at[i], count_r.at[i], *to))
+
+    def block_of(g):
+        return ((z + OFFSET[g] + NZ) % NZ) * NX
+
+    def move_tiles():
+        out = []
+        for n, g in enumerate(MOVED):
+            for dx in (2, 1, 3):
+                xx = (x + NX - dx) % NX
+                i = dx - 1
+                out.append(
+                    send(
+                        tiles_h.at[block_of(g) + xx],
+                        far_tiles.at[n, i],
+                        t_s.at[n, i],
+                        t_r.at[n, i],
+                        r,
+                        z,
+                        xx,
+                    )
+                )
+        return out
 
     def early1():
-        for copy in col_copies:
+        for copy in tables:
             copy.wait_recv()
-        fetch(7, far_v, far_s).wait()
+        copies = [
+            fetch(7, far_v, far_s),
+            fetch(9, far_rows_v, far_rows_s),
+            fetch(10, far_counts_v, far_counts_s),
+        ]
+        for copy in copies:
+            copy.wait()
+
+    moving = []
 
     kept = []
 
     def keep1():
+        moving.extend(move_tiles())
         kept.append(fetch(8, feat, raw[0][0].at[pl.ds(at, OWN)]))
 
     def ready1():
@@ -278,54 +322,93 @@
 
     def keep2():
         raw[1][0][pl.ds(at, OWN)] = agg1[...]
+
+    def place(into, at, tile, row, live, slot):
+        for b in range(OWN):
+            into[*at, b * TILE : (b + 1) * TILE, slot * TILE : (slot + 1) * TILE] = jnp.where(
+                jnp.logical_and(live, row == b), tile, jnp.zeros_like(tile)
+            )
 
     def meanwhile1():
         for copy in small + large:
             copy.wait()
         for g in range(GROUPS):
-            zc = (z + OFFSET[g] + NZ) % NZ
-
-            def place(xc, carry, g=g, zc=zc):
-                c = zc * NX + xc
-                for s in range(SLOTS):
-                    tile = tiles[c, s]
-                    row = rows_s[s, c]
-                    live = s < counts_s[c]
-                    for b in range(OWN):
-                        spread[g * NX + xc, b * TILE : (b + 1) * TILE, s * TILE : (s + 1) * TILE] = (
-                            jnp.where(jnp.logical_and(live, row == b), tile, jnp.zeros_like(tile))
-                        )
+
+            def body(xc, carry, g=g):
+                c = block_of(g) + xc
+                for t in range(SLOTS):
+                    place(spread, (g * NX + xc,), tiles[c, t], rows_s[t, c], t < counts_s[0, c], t)
                 return carry
 
-            lax.fori_loop(0, NX, place, 0)
+            lax.fori_loop(0, NX, body, 0)
         w_in_t[...] = w_in[...].astype(F32).T.astype(BF)
         dagg_t[...] = dot(w_out[...], cot[...], 1, 1).astype(BF)
         acc1[...] = jnp.zeros_like(acc1)
         acc2[...] = jnp.zeros_like(acc2)
         acc3[...] = jnp.zeros_like(acc3)
 
-    def consume1(g, xc):
-        near = picked[0][g, xc].reshape(SLOTS * TILE, TILE)
-        acc1[...] += dot(spread[g * NX + xc], near, 1, 0)
-
-    exchange(0, feat, keep1, ready1, early1, meanwhile1, consume1)
-    agg1[...] = acc1[...].astype(BF).reshape(OWN, TILE, TILE)
-
-    def consume2(g, xc):
-        near = picked[1][g, xc].reshape(SLOTS * TILE, TILE)
-        tile = spread[g * NX + xc]
-        z1 = dot(w_in_t[...], near, 1, 1)
-        sig = 0.5 + 0.5 * jnp.tanh(0.5 * z1)
-        hidden = z1 * sig
-        slope = sig + hidden * (1.0 - sig)
-        acc2[...] += dot(hidden.astype(BF), tile, 1, 1)
-        dz = (dot(dagg_t[...], tile, 1, 0) * slope).astype(BF)
-        acc3[...] += dot(dz, near, 1, 0)
-
-    def nothing():
+    def consume1(g, pieces):
+        total = acc1[...]
+        for xc in pieces:
+            near = picked[0][g, xc].reshape(SLOTS * TILE, TILE)
+            total = total + dot(spread[g * NX + xc], near, 1, 0)
+        acc1[...] = total
+
+    def middle1():
+        for copy in moving:
+            copy.wait_recv()
+        for n, g in enumerate(MOVED):
+            c = block_of(g) + x
+            for i in range(NX - 1):
+                for t in range(SLOTS):
+                    live = t < far_counts_s[i, 0, c]
+                    place(far_spread, (n, i), far_tiles[n, i, t], far_rows_s[i, t, c], live, t)
+
+    far_copies = []
+
+    def moved(g):
+        n = MOVED.index(g)
+        c = block_of(g) + x
+        for i in range(NX - 1):
+            for t in range(SLOTS):
+                far_near[i, t] = block(0, g, far_s[i, t, c])
+            term = dot(far_spread[n, i], far_near[i].reshape(SLOTS * TILE, TILE), 1, 0)
+            far_acc[i] = term if n == 0 else far_acc[i] + term
+        if n == len(MOVED) - 1:
+            far_out[...] = far_acc[...].astype(BF)
+            for dx in (2, 1, 3):
+                i = dx - 1
+                far_copies.append(
+                    send(far_out.at[i], far_in.at[i], f_s.at[i], f_r.at[i], r, z, (x + dx) % NX)
+                )
+        for t in range(SLOTS):
+            far_near[NX - 1, t] = block(0, g, cols_s[t, c])
+        near = far_near[NX - 1].reshape(SLOTS * TILE, TILE)
+        acc1[...] += dot(spread[g * NX + x], near, 1, 0)
+
+    def nothing(g=None):
         pass
 
-    exchange(1, agg1, keep2, nothing, nothing, nothing, consume2)
+    exchange(0, feat, keep1, ready1, early1, meanwhile1, middle1, consume1)
+    total = acc1[...]
+    for i, copy in enumerate(far_copies):
+        copy.wait_recv()
+        total = total + far_in[(1, 0, 2)[i]].astype(F32)
+    agg1[...] = total.astype(BF).reshape(OWN, TILE, TILE)
+
+    def consume2(g, pieces):
+        for xc in pieces:
+            near = picked[1][g, xc].reshape(SLOTS * TILE, TILE)
+            tile = spread[g * NX + xc]
+            z1 = dot(w_in_t[...], near, 1, 1)
+            sig = 0.5 + 0.5 * jnp.tanh(0.5 * z1)
+            hidden = z1 * sig
+            slope = sig + hidden * (1.0 - sig)
+            acc2[...] += dot(hidden.astype(BF), tile, 1, 1)
+            dz = (dot(dagg_t[...], tile, 1, 0) * slope).astype(BF)
+            acc3[...] += dot(dz, near, 1, 0)
+
+    exchange(1, agg1, keep2, nothing, nothing, nothing, nothing, consume2)
 
     agg2_t[...] = acc2[...].astype(BF)
 
@@ -417,7 +500,17 @@
         pltpu.VMEM((256, 512), BF),
         pltpu.SMEM((SLOTS, ND), jnp.int32),
         pltpu.SMEM((SLOTS, ND), jnp.int32),
-        pltpu.SMEM((ND,), jnp.int32),
+        pltpu.SMEM((1, ND), jnp.int32),
+        pltpu.VMEM((NX - 1, SLOTS, ND), jnp.int32),
+        pltpu.SMEM((NX - 1, SLOTS, ND), jnp.int32),
+        pltpu.VMEM((NX - 1, 1, ND), jnp.int32),
+        pltpu.SMEM((NX - 1, 1, ND), jnp.int32),
+        pltpu.VMEM((len(MOVED), NX - 1, SLOTS, TILE, TILE), BF),
+        pltpu.VMEM((len(MOVED), NX - 1, 256, 256), BF),
+        pltpu.VMEM((NX, SLOTS, TILE, TILE), BF),
+        pltpu.VMEM((NX - 1, 256, TILE), F32),
+        pltpu.VMEM((NX - 1, 256, TILE), BF),
+        pltpu.VMEM((NX - 1, 256, TILE), BF),
         pltpu.VMEM((NX - 1, SLOTS, ND), jnp.int32),
         pltpu.SMEM((NX - 1, SLOTS, ND), jnp.int32),
         pltpu.VMEM((ND, 256, 256), BF),
@@ -444,7 +537,9 @@
         (NX - 1,),
     ):
         scratch += [dma(shape)] * 2
-    scratch += [dma((9,))]
+    scratch += [dma((11,))]
+    for shape in ((len(MOVED), NX - 1), (NX - 1,), (NX - 1,), (NX - 1,)):
+        scratch += [dma(shape)] * 2
     for count in (1, PLANE - 1, NZ - 1, PLANE - 1, PLANE):
         scratch += [dma((count,))] * 2
     logits, full = pl.pallas_call(
@@ -466,7 +561,7 @@
         tile_values.reshape(ND, SLOTS, TILE, TILE),
         tile_rows[0, 0].T,
         tile_cols[0, 0].T,
-        tile_counts.reshape(ND),
+        tile_counts[0],
         features.reshape(OWN, TILE, TILE),
         weight_in,
         weight_out,

time: 111 us -> 105 us (0.946)
  Pallas kernels: 110 us -> 104 us
    pallas_call x1, Pallas kernels: 108 us -> 101 us  [per_device(): pl.pallas_call(kernel, out_shape=(jax.ShapeDtypeStruct((256, 512), BF), j...]
where the time goes in v4:
time: 105 us; the launch traced here: 104 us
  Pallas kernels  104 us (99%)
    pallas_call x1, Pallas kernels, per_device(): pl.pallas_call(kernel, out_shape=(jax.ShapeDtypeStruct((256, 512), BF), j...  101 us
    pallas_call x1, Pallas kernels, per_device(): pl.pallas_call(unpack, out_shape=(jax.ShapeDtypeStruct((256, 512), BF), j...  2.35 us

profile of v4, /device:TPU:1, one launch (start us, length us, event | category | flops | bytes accessed | tf_op | source)
XLA Modules:
  0.0 104.4 jit_solution(9474590867882706138)
XLA Ops:
  0.6 101.4 %shard_map.103 = (bf16[256,512]{1,0:T(8,128)(2,1)}, bf16[32,16,640]{2,1,0:T(8,128)(2,1)}) custom-call(bf16[32,2,128,128]{3,2,1,0:T(8,128)(2,1)} %bitcast.9, s32[2,32]{1,0:T(2,128)} %bitcast.11, s32[2,32]{1,0:T(2,128)} %bitcast.12, s32[1,32]{1,0:T(1,128)} %bitcast.13, bf16[2,128,128]{2,1,0:T(8,128)(2,1)} %bitcast.10, bf16[128,512]{1,0:T(8,128)(2,1)} %refs_5_.1, ...), custom_call_target="tpu_custom_call" | custom-call | flops 5000000000 | bytes 5000000 | tf_op jit(solution)/shard_map/pallas_call | solution.py:545
  102.0 2.4 %shard_map.104 = (bf16[256,512]{1,0:T(8,128)(2,1)}, f32[128,512]{1,0:T(8,128)}, f32[512,512]{1,0:T(8,128)}) custom-call(bf16[256,512]{1,0:T(8,128)(2,1)} %get-tuple-element.5.logits_in, bf16[32,16,640]{2,1,0:T(8,128)(2,1)} %get-tuple-element.6.full), custom_call_target="tpu_custom_call" | custom-call | tf_op jit(solution)/shard_map/pallas_call | solution.py:570

commit v5 on v4

--- a/solution.py
+++ b/solution.py
@@ -21,6 +21,7 @@
 GROUPS = NZ
 PLANE = NY * NX
 LANES = 640
+WIDE = 512
 CHUNK = 16
 CHUNKS = 512 // CHUNK
 SHARE = CHUNKS // NK
@@ -48,7 +49,7 @@
         return out
 
     tiles_h, rows_h, cols_h, counts_h, feat, w_in_h, w_out_h, cot_h = take(8)
-    logits_h, full_h = take(2)
+    logits_h, full_h, small_h = take(3)
     raw = [take(GROUPS), take(GROUPS)]
     picked = take(2)
     sending = take(2)
@@ -57,17 +58,16 @@
     far_tiles, far_spread, far_near, far_acc, far_out, far_in = take(6)
     far_v, far_s, spread, w_in_t, dagg_t, acc1, agg1, acc2, acc3 = take(9)
     agg2_t, logits, red1_out, red1_in, red2_out, red2_in, red3, full = take(8)
-    y_s, y_r, b_s, b_r, p_s, p_r, c_s, c_r, col_s, col_r, loc = take(11)
-    t_s, t_r, row_s, row_r, count_s, count_r, f_s, f_r = take(8)
-    g1_s, g1_r, g2_s, g2_r, g3_s, g3_r, g4_s, g4_r, g5_s, g5_r = take(10)
+    low_out, low_in, low_sum, low_full = take(4)
+    sent, y_r, piece_r, b_r, p_r, c_r, last_r, col_s, col_r, row_s, row_r = take(11)
+    count_s, count_r, t_r, f_r, ar_r, g4_r, loc = take(7)
 
     r = lax.axis_index("rep")
     d = lax.axis_index("dom")
     y, k = r // NK, r % NK
     z, x = d // NX, d % NX
-    left = []
-
-    def send(src, dst, s_sem, r_sem, rr, zz, xx):
+
+    def copy_to(src, dst, s_sem, r_sem, rr, zz, xx):
         copy = pltpu.make_async_remote_copy(
             src_ref=src,
             dst_ref=dst,
@@ -77,8 +77,13 @@
             device_id_type=pl.DeviceIdType.MESH,
         )
         copy.start()
-        left.append(copy)
         return copy
+
+    def wait_bytes(like, sem):
+        pltpu.make_async_copy(like, like, sem).wait()
+
+    def send(src, dst, kind, r_sem, rr, zz, xx):
+        return copy_to(src, dst, sent.at[kind], r_sem, rr, zz, xx)
 
     def fetch(i, src, dst):
         copy = pltpu.make_async_copy(src, dst, loc.at[i])
@@ -94,12 +99,9 @@
     ]
 
     greet = [(y * NK + 1 - k, z, x)]
-    for dx in range(NX):
-        for dy in range(NY):
-            if dx or dy:
-                greet.append((((y + dy) % NY) * NK + k, z, (x + dx) % NX))
-    for dz in range(1, NZ):
-        greet.append((r, (z + dz) % NZ, x))
+    greet += [(((y + dy) % NY) * NK + k, z, x) for dy in range(1, NY)]
+    greet += [(r, z, (x + dx) % NX) for dx in range(1, NX)]
+    greet += [(r, (z + dz) % NZ, x) for dz in (1, NZ - 1)]
     barrier = pltpu.get_barrier_semaphore()
     for rr, zz, xx in greet:
         pl.semaphore_signal(
@@ -117,8 +119,8 @@
         return send(
             src,
             raw[p][group_of(way, step)].at[here],
-            b_s.at[p, way, step - 1],
-            b_r.at[p, way, step - 1],
+            2 + p,
+            b_r.at[p, step - 1],
             r,
             (z + (1, NZ - 1)[way]) % NZ,
             x,
@@ -130,8 +132,8 @@
             send(
                 own if g == 0 else raw[p][g].at[here],
                 raw[p][g].at[here],
-                y_s.at[p, g, dy - 1],
-                y_r.at[p, g, dy - 1],
+                p,
+                piece_r.at[p, g - 1, dy - 1] if g in (1, 2) else y_r.at[p, g],
                 ((y + dy) % NY) * NK + k,
                 z,
                 x,
@@ -145,8 +147,8 @@
         return send(
             raw[p][group_of(way, 1)].at[here],
             raw[p][g].at[here],
-            y_s.at[p, g, i - 1],
-            y_r.at[p, g, i - 1],
+            p,
+            y_r.at[p, g],
             r,
             (z + (1, NZ - 1)[way]) % NZ,
             x,
@@ -156,7 +158,7 @@
         return send(
             raw[p][g].at[half],
             raw[p][g].at[half],
-            p_s.at[p, g],
+            4 + p,
             p_r.at[p, g],
             y * NK + 1 - k,
             z,
@@ -176,8 +178,8 @@
                 send(
                     sending[p].at[g, dx - 1],
                     picked[p].at[g, x],
-                    c_s.at[p, g, dx - 1],
-                    c_r.at[p, g, dx - 1],
+                    6 + p,
+                    last_r.at[dx - 1] if p == 1 and g == GROUPS - 1 else c_r.at[p, g],
                     r,
                     z,
                     (x + dx) % NX,
@@ -194,8 +196,7 @@
         keep()
 
         def do_z(step):
-            for copy in rings[step - 1]:
-                copy.wait_recv()
+            wait_bytes(raw[p][0].at[pl.ds(0, 2 * OWN if step < STEPS else OWN)], b_r.at[p, step - 1])
             if step < STEPS:
                 rings[step] = [ring(p, own, 0, step + 1), ring(p, own, 1, step + 1)]
             for g in sorted({group_of(0, step), group_of(1, step)}):
@@ -203,10 +204,12 @@
                     ys[g] = gather_y(p, own, g)
 
         def do_y(g):
-            for i, copy in enumerate(ys[g]):
-                copy.wait_recv()
-                if g in (1, 2):
-                    ys.setdefault(g + 2, []).append(relay(p, g - 1, i + 1))
+            if g in (1, 2):
+                for i, copy in enumerate(ys[g]):
+                    copy.wait_recv()
+                    relay(p, g - 1, i + 1)
+            else:
+                wait_bytes(raw[p][g].at[pl.ds(0, (NY - 1) * OWN)], y_r.at[p, g])
             if g == 0:
                 ready()
             shares[g] = share(p, g)
@@ -216,8 +219,7 @@
             picks[g] = pick(p, g)
 
         def do_c(g):
-            for copy in picks[g]:
-                copy.wait_recv()
+            wait_bytes(sending[p].at[g], c_r.at[p, g])
             consume(g, range(NX))
 
         def do_last(g):
@@ -272,31 +274,19 @@
     for dx in range(1, NX):
         to = (r, z, (x + NX - dx) % NX)
         i = dx - 1
-        tables.append(send(cols_h, far_v.at[i], col_s.at[i], col_r.at[i], *to))
-        tables.append(send(rows_h, far_rows_v.at[i], row_s.at[i], row_r.at[i], *to))
-        tables.append(send(counts_h, far_counts_v.at[i], count_s.at[i], count_r.at[i], *to))
+        tables.append(copy_to(cols_h, far_v.at[i], col_s.at[i], col_r.at[i], *to))
+        tables.append(copy_to(rows_h, far_rows_v.at[i], row_s.at[i], row_r.at[i], *to))
+        tables.append(copy_to(counts_h, far_counts_v.at[i], count_s.at[i], count_r.at[i], *to))
 
     def block_of(g):
         return ((z + OFFSET[g] + NZ) % NZ) * NX
 
     def move_tiles():
-        out = []
         for n, g in enumerate(MOVED):
             for dx in (2, 1, 3):
                 xx = (x + NX - dx) % NX
-                i = dx - 1
-                out.append(
-                    send(
-                        tiles_h.at[block_of(g) + xx],
-                        far_tiles.at[n, i],
-                        t_s.at[n, i],
-                        t_r.at[n, i],
-                        r,
-                        z,
-                        xx,
-                    )
-                )
-        return out
+                tile = tiles_h.at[block_of(g) + xx]
+                send(tile, far_tiles.at[n, dx - 1], 8, t_r.at[0], r, z, xx)
 
     def early1():
         for copy in tables:
@@ -309,12 +299,10 @@
         for copy in copies:
             copy.wait()
 
-    moving = []
-
     kept = []
 
     def keep1():
-        moving.extend(move_tiles())
+        move_tiles()
         kept.append(fetch(8, feat, raw[0][0].at[pl.ds(at, OWN)]))
 
     def ready1():
@@ -355,16 +343,13 @@
         acc1[...] = total
 
     def middle1():
-        for copy in moving:
-            copy.wait_recv()
+        wait_bytes(far_tiles, t_r.at[0])
         for n, g in enumerate(MOVED):
             c = block_of(g) + x
             for i in range(NX - 1):
                 for t in range(SLOTS):
                     live = t < far_counts_s[i, 0, c]
                     place(far_spread, (n, i), far_tiles[n, i, t], far_rows_s[i, t, c], live, t)
-
-    far_copies = []
 
     def moved(g):
         n = MOVED.index(g)
@@ -378,9 +363,7 @@
             far_out[...] = far_acc[...].astype(BF)
             for dx in (2, 1, 3):
                 i = dx - 1
-                far_copies.append(
-                    send(far_out.at[i], far_in.at[i], f_s.at[i], f_r.at[i], r, z, (x + dx) % NX)
-                )
+                send(far_out.at[i], far_in.at[i], 9, f_r.at[0], r, z, (x + dx) % NX)
         for t in range(SLOTS):
             far_near[NX - 1, t] = block(0, g, cols_s[t, c])
         near = far_near[NX - 1].reshape(SLOTS * TILE, TILE)
@@ -391,9 +374,9 @@
 
     exchange(0, feat, keep1, ready1, early1, meanwhile1, middle1, consume1)
     total = acc1[...]
-    for i, copy in enumerate(far_copies):
-        copy.wait_recv()
-        total = total + far_in[(1, 0, 2)[i]].astype(F32)
+    wait_bytes(far_in, f_r.at[0])
+    for i in range(NX - 1):
+        total = total + far_in[i].astype(F32)
     agg1[...] = total.astype(BF).reshape(OWN, TILE, TILE)
 
     def consume2(g, pieces):
@@ -422,65 +405,106 @@
     out, back = term(1 - k)
     red1_out[:, :, 0:512] = out.astype(BF)
     red1_out[:, :, 512:LANES] = back.astype(BF)
-    copy = send(red1_out, red1_in, g1_s.at[0], g1_r.at[0], y * NK + 1 - k, z, x)
+    copy = send(red1_out, red1_in, 10, ar_r.at[0], y * NK + 1 - k, z, x)
     out, back = term(k)
     copy.wait_recv()
-    red2_out[:, :, 0:512] = (out + red1_in[:, :, 0:512].astype(F32)).astype(BF)
-    red2_out[:, :, 512:LANES] = (back + red1_in[:, :, 512:LANES].astype(F32)).astype(BF)
+    red2_out[...] = (out + red1_in[:, :, 0:WIDE].astype(F32)).astype(BF)
+    low_out[...] = (back + red1_in[:, :, WIDE:LANES].astype(F32)).astype(BF)
+
     me = y * NX + x
     plane = [(dy, dx) for dy in range(NY) for dx in range(NX) if dy or dx]
     plane.sort(key=lambda step: -min(step[0], NY - step[0]) - min(step[1], NX - step[1]))
-    copies = []
-    for i, (dy, dx) in enumerate(plane):
-        yy, xx = (y + dy) % NY, (x + dx) % NX
-        copies.append(
-            send(red2_out.at[yy * NX + xx], red2_in.at[i], g2_s.at[i], g2_r.at[i], yy * NK + k, z, xx)
-        )
+    there = [((y + dy) % NY, (x + dx) % NX) for dy, dx in plane]
+    along = [(z + i) % NZ for i in (4, 3, 5, 2, 6, 1, 7)]
+    for i, (yy, xx) in enumerate(there):
+        send(red2_out.at[yy * NX + xx], red2_in.at[i], 11, ar_r.at[1], yy * NK + k, z, xx)
+    for i, zz in enumerate(along):
+        send(low_out.at[pl.ds(2 * zz, 2)], low_in.at[i], 12, ar_r.at[2], r, zz, x)
     logits[...] = dot(agg2_t[...], w_out[...], 0, 0).astype(BF)
     done = fetch(0, logits, logits_h)
+
+    wait_bytes(low_in, ar_r.at[2])
+    total = low_out[pl.ds(2 * z, 2)].astype(F32)
+    for i in range(NZ - 1):
+        total = total + low_in[i].astype(F32)
+    low_sum[me] = total.astype(BF)
+    for yy, xx in there:
+        send(low_sum.at[me], low_sum.at[me], 13, ar_r.at[3], yy * NK + k, z, xx)
+
+    wait_bytes(red2_in, ar_r.at[1])
     total = red2_out[me].astype(F32)
-    for i in range(PLANE - 2, -1, -1):
-        copies[i].wait_recv()
+    for i in range(PLANE - 1):
         total = total + red2_in[i].astype(F32)
     red3[z] = total.astype(BF)
-    copies = [
-        send(red3.at[z], red3.at[z], g3_s.at[i - 1], g3_r.at[i - 1], r, (z + i) % NZ, x)
-        for i in (4, 3, 5, 2, 6, 1, 7)
-    ]
-    for copy in copies:
-        copy.wait_recv()
+    for zz in along:
+        send(red3.at[z], red3.at[z], 14, ar_r.at[4], r, zz, x)
+
+    wait_bytes(low_sum.at[pl.ds(0, PLANE - 1)], ar_r.at[3])
+    total = low_sum[0].astype(F32)
+    for i in range(1, PLANE):
+        total = total + low_sum[i].astype(F32)
+    here = pl.ds(SHARE * k + 2 * z, 2)
+    low_full[here] = total.astype(BF)
+    for zz in along:
+        send(low_full.at[here], low_full.at[here], 15, ar_r.at[5], r, zz, x)
+
+    wait_bytes(red3.at[pl.ds(0, NZ - 1)], ar_r.at[4])
     total = red3[0].astype(F32)
     for i in range(1, NZ):
         total = total + red3[i].astype(F32)
-
-    def to_core(i, chunk):
-        return send(chunk, chunk, g5_s.at[i], g5_r.at[i], y * NK + 1 - k, z, x)
-
     full[SHARE * k + me] = total.astype(BF)
     chunk = full.at[SHARE * k + me]
-    copies = []
-    for i, (dy, dx) in enumerate(plane):
-        yy, xx = (y + dy) % NY, (x + dx) % NX
-        copies.append(send(chunk, chunk, g4_s.at[i], g4_r.at[i], yy * NK + k, z, xx))
-    others = [to_core(PLANE - 1, chunk)]
+    copies = [
+        send(chunk, chunk, 16, g4_r.at[i], yy * NK + k, z, xx) for i, (yy, xx) in enumerate(there)
+    ]
+
+    def to_core(chunk, n):
+        return send(chunk, chunk, 17 + n, ar_r.at[6 + n], y * NK + 1 - k, z, x)
+
+    to_core(chunk, 0)
+    wait_bytes(low_full.at[pl.ds(0, 2 * (NZ - 1))], ar_r.at[5])
+    mine = pl.ds(SHARE * k, SHARE)
+    to_core(low_full.at[mine], 1)
     for i in range(PLANE - 2, -1, -1):
         copies[i].wait_recv()
         dy, dx = plane[i]
         came = ((y + NY - dy) % NY) * NX + (x + NX - dx) % NX
-        others.append(to_core(i, full.at[SHARE * k + came]))
-    for copy in others:
-        copy.wait_recv()
-    last = fetch(1, full, full_h)
-    for copy in left:
+        to_core(full.at[SHARE * k + came], 0)
+    half_full = full.at[mine]
+    half_low = low_full.at[mine]
+    wait_bytes(half_low, ar_r.at[7])
+    last = [fetch(2, low_full, small_h)]
+    wait_bytes(half_full, ar_r.at[6])
+    last.append(fetch(1, full, full_h))
+
+    for copy in tables:
         copy.wait_send()
+    for p in range(2):
+        wait_bytes(sending[p], sent.at[p])
+        wait_bytes(raw[p][0].at[pl.ds(0, 2 * OWN * (STEPS - 1) + OWN)], sent.at[2 + p])
+        wait_bytes(picked[p], sent.at[4 + p])
+    wait_bytes(sending[0].at[pl.ds(0, GROUPS - len(MOVED))], sent.at[6])
+    wait_bytes(sending[1], sent.at[7])
+    wait_bytes(far_tiles, sent.at[8])
+    wait_bytes(far_out, sent.at[9])
+    wait_bytes(red1_out, sent.at[10])
+    wait_bytes(red2_in, sent.at[11])
+    wait_bytes(low_in, sent.at[12])
+    wait_bytes(low_sum.at[pl.ds(0, PLANE - 1)], sent.at[13])
+    wait_bytes(red3.at[pl.ds(0, NZ - 1)], sent.at[14])
+    wait_bytes(low_full.at[pl.ds(0, 2 * (NZ - 1))], sent.at[15])
+    wait_bytes(red2_in, sent.at[16])
+    wait_bytes(half_full, sent.at[17])
+    wait_bytes(half_low, sent.at[18])
     done.wait()
-    last.wait()
-
-
-def unpack(logits_in, full, logits, grad_in, grad_out):
+    for copy in last:
+        copy.wait()
+
+
+def unpack(logits_in, full, low, logits, grad_in, grad_out):
     logits[...] = logits_in[...]
-    grad_out[...] = full[:, :, 0:512].astype(F32).reshape(512, 512)
-    grad_in[...] = full[:, :, 512:LANES].astype(F32).reshape(512, TILE).T
+    grad_out[...] = full[...].astype(F32).reshape(512, WIDE)
+    grad_in[...] = low[...].astype(F32).reshape(512, TILE).T
 
 
 def per_device(
@@ -524,32 +548,36 @@
         pltpu.VMEM((256, 512), BF),
         pltpu.VMEM((SHARE, CHUNK, LANES), BF),
         pltpu.VMEM((SHARE, CHUNK, LANES), BF),
-        pltpu.VMEM((SHARE, CHUNK, LANES), BF),
-        pltpu.VMEM((PLANE - 1, CHUNK, LANES), BF),
-        pltpu.VMEM((NZ, CHUNK, LANES), BF),
-        pltpu.VMEM((CHUNKS, CHUNK, LANES), BF),
+        pltpu.VMEM((SHARE, CHUNK, WIDE), BF),
+        pltpu.VMEM((PLANE - 1, CHUNK, WIDE), BF),
+        pltpu.VMEM((NZ, CHUNK, WIDE), BF),
+        pltpu.VMEM((CHUNKS, CHUNK, WIDE), BF),
+        pltpu.VMEM((SHARE, CHUNK, TILE), BF),
+        pltpu.VMEM((NZ - 1, 2, CHUNK, TILE), BF),
+        pltpu.VMEM((PLANE, 2, CHUNK, TILE), BF),
+        pltpu.VMEM((CHUNKS, CHUNK, TILE), BF),
     ]
     for shape in (
-        (2, GROUPS, NY - 1),
-        (2, 2, STEPS),
+        (19,),
         (2, GROUPS),
-        (2, GROUPS, NX - 1),
+        (2, 2, NY - 1),
+        (2, STEPS),
+        (2, GROUPS),
+        (2, GROUPS),
         (NX - 1,),
     ):
-        scratch += [dma(shape)] * 2
-    scratch += [dma((11,))]
-    for shape in ((len(MOVED), NX - 1), (NX - 1,), (NX - 1,), (NX - 1,)):
-        scratch += [dma(shape)] * 2
-    for count in (1, PLANE - 1, NZ - 1, PLANE - 1, PLANE):
-        scratch += [dma((count,))] * 2
-    logits, full = pl.pallas_call(
+        scratch.append(dma(shape))
+    scratch += [dma((NX - 1,))] * 6
+    scratch += [dma((1,)), dma((1,)), dma((8,)), dma((PLANE - 1,)), dma((11,))]
+    logits, full, low = pl.pallas_call(
         kernel,
         out_shape=(
             jax.ShapeDtypeStruct((256, 512), BF),
-            jax.ShapeDtypeStruct((CHUNKS, CHUNK, LANES), BF),
+            jax.ShapeDtypeStruct((CHUNKS, CHUNK, WIDE), BF),
+            jax.ShapeDtypeStruct((CHUNKS, CHUNK, TILE), BF),
         ),
         in_specs=[hbm] * 8,
-        out_specs=(hbm,) * 2,
+        out_specs=(hbm,) * 3,
         scratch_shapes=scratch,
         compiler_params=pltpu.CompilerParams(
             collective_id=0, has_side_effects=True, vmem_limit_bytes=60 * 1024 * 1024
@@ -574,10 +602,10 @@
             jax.ShapeDtypeStruct((TILE, 512), F32),
             jax.ShapeDtypeStruct((512, 512), F32),
         ),
-        in_specs=[vmem, vmem],
+        in_specs=[vmem] * 3,
         out_specs=(vmem, vmem, vmem),
         compiler_params=pltpu.CompilerParams(vmem_limit_bytes=60 * 1024 * 1024),
-    )(logits, full)
+    )(logits, full, low)
 
 
 def solution(mesh):

time: 105 us -> 99.1 us (0.944)
  Pallas kernels: 104 us -> 98.4 us
    pallas_call x1, Pallas kernels: 101 us -> 96.1 us  [per_device(): pl.pallas_call(kernel, out_shape=(jax.ShapeDtypeStruct((256, 512), BF), j...]
where the time goes in v5:
time: 99.1 us; the launch traced here: 99 us
  Pallas kernels  98.4 us (99%)
    pallas_call x1, Pallas kernels, per_device(): pl.pallas_call(kernel, out_shape=(jax.ShapeDtypeStruct((256, 512), BF), j...  96.1 us
    pallas_call x1, Pallas kernels, per_device(): pl.pallas_call(unpack, out_shape=(jax.ShapeDtypeStruct((256, 512), BF), j...  2.32 us

profile of v5, /device:TPU:1, one launch (start us, length us, event | category | flops | bytes accessed | tf_op | source)
XLA Modules:
  0.0 99.0 jit_solution(8167231100627520735)
XLA Ops:
  0.6 96.1 %shard_map.103 = (bf16[256,512]{1,0:T(8,128)(2,1)}, bf16[32,16,512]{2,1,0:T(8,128)(2,1)}, bf16[32,16,128]{2,1,0:T(8,128)(2,1)}) custom-call(bf16[32,2,128,128]{3,2,1,0:T(8,128)(2,1)} %bitcast.9, s32[2,32]{1,0:T(2,128)} %bitcast.11, s32[2,32]{1,0:T(2,128)} %bitcast.12, s32[1,32]{1,0:T(1,128)} %bitcast.13, bf16[2,128,128]{2,1,0:T(8,128)(2,1)} %bitcast.10, ...), custom_call_target="tpu_custom_call" | custom-call | flops 5000000000 | bytes 5000000 | tf_op jit(solution)/shard_map/pallas_call | solution.py:572
  96.7 2.3 %shard_map.104 = (bf16[256,512]{1,0:T(8,128)(2,1)}, f32[128,512]{1,0:T(8,128)}, f32[512,512]{1,0:T(8,128)}) custom-call(bf16[256,512]{1,0:T(8,128)(2,1)} %get-tuple-element.6.logits_in, bf16[32,16,512]{2,1,0:T(8,128)(2,1)} %get-tuple-element.7.full, bf16[32,16,128]{2,1,0:T(8,128)(2,1)} %get-tuple-element.8.low), custom_call_target="tpu_custom_call" | custom-call | tf_op jit(solution)/shard_map/pallas_call | solution.py:598

commit v6 on v5

--- a/solution.py
+++ b/solution.py
@@ -16,10 +16,13 @@
 OWN = 2
 BLOCKS = NR * OWN
 HALF = BLOCKS // NK
-MOVED = (6, 7)
+EARLY = (0, 1, 2)
+LAST = 5
+MOVED = (6, 7, LAST)
 STEPS = NZ // 2
 GROUPS = NZ
 PLANE = NY * NX
+FAR_FIRST = (2, 1, 3)
 LANES = 640
 WIDE = 512
 CHUNK = 16
@@ -133,19 +136,19 @@
                 own if g == 0 else raw[p][g].at[here],
                 raw[p][g].at[here],
                 p,
-                piece_r.at[p, g - 1, dy - 1] if g in (1, 2) else y_r.at[p, g],
+                piece_r.at[p, g, dy - 1] if g in EARLY else y_r.at[p, g],
                 ((y + dy) % NY) * NK + k,
                 z,
                 x,
             )
-            for dy in range(1, NY)
+            for dy in FAR_FIRST
         ]
 
-    def relay(p, way, i):
+    def relay(p, way, step, i):
         here = pl.ds(HALF * k + OWN * ((y + NY - i) % NY), OWN)
-        g = group_of(way, 2)
+        g = group_of(way, step)
         return send(
-            raw[p][group_of(way, 1)].at[here],
+            raw[p][group_of(way, step - 1)].at[here],
             raw[p][g].at[here],
             p,
             y_r.at[p, g],
@@ -165,13 +168,18 @@
             x,
         )
 
+    def share_piece(p, g, dy, src=None):
+        here = pl.ds(HALF * k + OWN * ((y + NY - dy) % NY), OWN)
+        piece = raw[p][g].at[here]
+        send(piece if src is None else src, piece, 4 + p, p_r.at[p, g], y * NK + 1 - k, z, x)
+
     def block(p, g, j):
         return raw[p][g][((j >> 1) & 1) * HALF + (j >> 2) * OWN + (j & 1)]
 
     def pick(p, g):
         c = ((z + OFFSET[g] + NZ) % NZ) * NX + x
         copies = []
-        for dx in (2, 1, 3):
+        for dx in FAR_FIRST:
             for s in range(SLOTS):
                 sending[p][g, dx - 1, s] = block(p, g, far_s[dx - 1, s, c])
             copies.append(
@@ -179,7 +187,7 @@
                     sending[p].at[g, dx - 1],
                     picked[p].at[g, x],
                     6 + p,
-                    last_r.at[dx - 1] if p == 1 and g == GROUPS - 1 else c_r.at[p, g],
+                    last_r.at[dx - 1] if p == 1 and g == LAST else c_r.at[p, g],
                     r,
                     z,
                     (x + dx) % NX,
@@ -193,6 +201,7 @@
         rings = {0: [ring(p, own, 0, 1), ring(p, own, 1, 1)]}
         ys = {0: gather_y(p, own, 0)}
         shares, picks = {}, {}
+        share_piece(p, 0, 0, own)
         keep()
 
         def do_z(step):
@@ -200,22 +209,32 @@
             if step < STEPS:
                 rings[step] = [ring(p, own, 0, step + 1), ring(p, own, 1, step + 1)]
             for g in sorted({group_of(0, step), group_of(1, step)}):
-                if step != 2:
+                if step != 2 and g != LAST:
                     ys[g] = gather_y(p, own, g)
+                if g in EARLY:
+                    share_piece(p, g, 0)
 
         def do_y(g):
-            if g in (1, 2):
-                for i, copy in enumerate(ys[g]):
+            if g in EARLY:
+                for dy, copy in zip(FAR_FIRST, ys[g]):
                     copy.wait_recv()
-                    relay(p, g - 1, i + 1)
+                    share_piece(p, g, dy)
+                    if g > 0:
+                        relay(p, g - 1, 2, dy)
             else:
                 wait_bytes(raw[p][g].at[pl.ds(0, (NY - 1) * OWN)], y_r.at[p, g])
+                shares[g] = share(p, g)
+            if g == group_of(0, 2):
+                for dy in FAR_FIRST:
+                    relay(p, 0, 3, dy)
+
+        def do_k(g):
+            if g in EARLY:
+                wait_bytes(raw[p][g].at[half], p_r.at[p, g])
+            else:
+                shares[g].wait_recv()
             if g == 0:
                 ready()
-            shares[g] = share(p, g)
-
-        def do_k(g):
-            shares[g].wait_recv()
             picks[g] = pick(p, g)
 
         def do_c(g):
@@ -253,22 +272,22 @@
         do_z(4)
         do_w(3)
         do_c(0)
-        do_y(5)
-        do_w(5)
         do_y(4)
         do_w(4)
-        do_c(1)
         do_y(6)
         do_w(6)
-        do_c(2)
+        do_c(1)
         do_y(7)
         do_w(7)
+        do_c(2)
+        do_y(LAST)
+        do_w(LAST)
         do_c(3)
-        do_c(5)
         do_c(4)
         if p == 1:
             do_c(6)
-            do_last(7)
+            do_c(7)
+            do_last(LAST)
 
     tables = []
     for dx in range(1, NX):
@@ -458,24 +477,24 @@
         send(chunk, chunk, 16, g4_r.at[i], yy * NK + k, z, xx) for i, (yy, xx) in enumerate(there)
     ]
 
-    def to_core(chunk, n):
-        return send(chunk, chunk, 17 + n, ar_r.at[6 + n], y * NK + 1 - k, z, x)
-
-    to_core(chunk, 0)
+    def to_core(src, dst, n):
+        return send(src, dst, 17 + n, ar_r.at[6 + n], y * NK + 1 - k, z, x)
+
+    to_core(chunk, full_h.at[SHARE * k + me], 0)
     wait_bytes(low_full.at[pl.ds(0, 2 * (NZ - 1))], ar_r.at[5])
     mine = pl.ds(SHARE * k, SHARE)
-    to_core(low_full.at[mine], 1)
+    to_core(low_full.at[mine], small_h.at[mine], 1)
+    last = [fetch(2, low_full.at[mine], small_h.at[mine])]
     for i in range(PLANE - 2, -1, -1):
         copies[i].wait_recv()
         dy, dx = plane[i]
         came = ((y + NY - dy) % NY) * NX + (x + NX - dx) % NX
-        to_core(full.at[SHARE * k + came], 0)
+        to_core(full.at[SHARE * k + came], full_h.at[SHARE * k + came], 0)
     half_full = full.at[mine]
     half_low = low_full.at[mine]
+    last.append(fetch(1, half_full, full_h.at[mine]))
     wait_bytes(half_low, ar_r.at[7])
-    last = [fetch(2, low_full, small_h)]
     wait_bytes(half_full, ar_r.at[6])
-    last.append(fetch(1, full, full_h))
 
     for copy in tables:
         copy.wait_send()
@@ -560,7 +579,7 @@
     for shape in (
         (19,),
         (2, GROUPS),
-        (2, 2, NY - 1),
+        (2, len(EARLY), NY - 1),
         (2, STEPS),
         (2, GROUPS),
         (2, GROUPS),

time: 99.1 us -> 96.8 us (0.977)
  Pallas kernels: 98.4 us -> 96 us
    pallas_call x1, Pallas kernels: 96.1 us -> 93.7 us  [per_device(): pl.pallas_call(kernel, out_shape=(jax.ShapeDtypeStruct((256, 512), BF), j...]
where the time goes in v6:
time: 96.8 us; the launch traced here: 96.6 us
  Pallas kernels  96 us (99%)
    pallas_call x1, Pallas kernels, per_device(): pl.pallas_call(kernel, out_shape=(jax.ShapeDtypeStruct((256, 512), BF), j...  93.7 us
    pallas_call x1, Pallas kernels, per_device(): pl.pallas_call(unpack, out_shape=(jax.ShapeDtypeStruct((256, 512), BF), j...  2.32 us

profile of v6, /device:TPU:1, one launch (start us, length us, event | category | flops | bytes accessed | tf_op | source)
XLA Modules:
  0.0 96.6 jit_solution(10296669606583252807)
XLA Ops:
  0.6 93.7 %shard_map.103 = (bf16[256,512]{1,0:T(8,128)(2,1)}, bf16[32,16,512]{2,1,0:T(8,128)(2,1)}, bf16[32,16,128]{2,1,0:T(8,128)(2,1)}) custom-call(bf16[32,2,128,128]{3,2,1,0:T(8,128)(2,1)} %bitcast.9, s32[2,32]{1,0:T(2,128)} %bitcast.11, s32[2,32]{1,0:T(2,128)} %bitcast.12, s32[1,32]{1,0:T(1,128)} %bitcast.13, bf16[2,128,128]{2,1,0:T(8,128)(2,1)} %bitcast.10, ...), custom_call_target="tpu_custom_call" | custom-call | flops 5000000000 | bytes 5000000 | tf_op jit(solution)/shard_map/pallas_call | solution.py:591
  94.3 2.3 %shard_map.104 = (bf16[256,512]{1,0:T(8,128)(2,1)}, f32[128,512]{1,0:T(8,128)}, f32[512,512]{1,0:T(8,128)}) custom-call(bf16[256,512]{1,0:T(8,128)(2,1)} %get-tuple-element.6.logits_in, bf16[32,16,512]{2,1,0:T(8,128)(2,1)} %get-tuple-element.7.full, bf16[32,16,128]{2,1,0:T(8,128)(2,1)} %get-tuple-element.8.low), custom_call_target="tpu_custom_call" | custom-call | tf_op jit(solution)/shard_map/pallas_call | solution.py:617

commit v7 on v6

--- a/solution.py
+++ b/solution.py
@@ -174,7 +174,7 @@
         send(piece if src is None else src, piece, 4 + p, p_r.at[p, g], y * NK + 1 - k, z, x)
 
     def block(p, g, j):
-        return raw[p][g][((j >> 1) & 1) * HALF + (j >> 2) * OWN + (j & 1)]
+        return raw[p][g][((j >> 1) & 1) * HALF + ((j >> 2) & (NY - 1)) * OWN + (j & 1)]
 
     def pick(p, g):
         c = ((z + OFFSET[g] + NZ) % NZ) * NX + x
@@ -373,15 +373,16 @@
     def moved(g):
         n = MOVED.index(g)
         c = block_of(g) + x
-        for i in range(NX - 1):
+        for dx in FAR_FIRST:
+            i = dx - 1
             for t in range(SLOTS):
                 far_near[i, t] = block(0, g, far_s[i, t, c])
             term = dot(far_spread[n, i], far_near[i].reshape(SLOTS * TILE, TILE), 1, 0)
-            far_acc[i] = term if n == 0 else far_acc[i] + term
-        if n == len(MOVED) - 1:
-            far_out[...] = far_acc[...].astype(BF)
-            for dx in (2, 1, 3):
-                i = dx - 1
+            term = term if n == 0 else far_acc[i] + term
+            if n < len(MOVED) - 1:
+                far_acc[i] = term
+            else:
+                far_out[i] = term.astype(BF)
                 send(far_out.at[i], far_in.at[i], 9, f_r.at[0], r, z, (x + dx) % NX)
         for t in range(SLOTS):
             far_near[NX - 1, t] = block(0, g, cols_s[t, c])

time: 96.8 us -> 97 us (level)
  no operation moved by 1% of the time
where the time goes in v7:
time: 97 us; the launch traced here: 96.9 us
  Pallas kernels  96.2 us (99%)
    pallas_call x1, Pallas kernels, per_device(): pl.pallas_call(kernel, out_shape=(jax.ShapeDtypeStruct((256, 512), BF), j...  93.9 us
    pallas_call x1, Pallas kernels, per_device(): pl.pallas_call(unpack, out_shape=(jax.ShapeDtypeStruct((256, 512), BF), j...  2.32 us

profile of v7, /device:TPU:1, one launch (start us, length us, event | category | flops | bytes accessed | tf_op | source)
XLA Modules:
  0.0 96.9 jit_solution(14164979604255403181)
XLA Ops:
  0.6 93.9 %shard_map.103 = (bf16[256,512]{1,0:T(8,128)(2,1)}, bf16[32,16,512]{2,1,0:T(8,128)(2,1)}, bf16[32,16,128]{2,1,0:T(8,128)(2,1)}) custom-call(bf16[32,2,128,128]{3,2,1,0:T(8,128)(2,1)} %bitcast.9, s32[2,32]{1,0:T(2,128)} %bitcast.11, s32[2,32]{1,0:T(2,128)} %bitcast.12, s32[1,32]{1,0:T(1,128)} %bitcast.13, bf16[2,128,128]{2,1,0:T(8,128)(2,1)} %bitcast.10, ...), custom_call_target="tpu_custom_call" | custom-call | flops 5000000000 | bytes 5000000 | tf_op jit(solution)/shard_map/pallas_call | solution.py:592
  94.5 2.3 %shard_map.104 = (bf16[256,512]{1,0:T(8,128)(2,1)}, f32[128,512]{1,0:T(8,128)}, f32[512,512]{1,0:T(8,128)}) custom-call(bf16[256,512]{1,0:T(8,128)(2,1)} %get-tuple-element.6.logits_in, bf16[32,16,512]{2,1,0:T(8,128)(2,1)} %get-tuple-element.7.full, bf16[32,16,128]{2,1,0:T(8,128)(2,1)} %get-tuple-element.8.low), custom_call_target="tpu_custom_call" | custom-call | tf_op jit(solution)/shard_map/pallas_call | solution.py:618

commit v8 on v7

--- a/solution.py
+++ b/solution.py
@@ -523,14 +523,13 @@
 
 def unpack(logits_in, full, low, logits, grad_in, grad_out):
     logits[...] = logits_in[...]
-    grad_out[...] = full[...].astype(F32).reshape(512, WIDE)
-    grad_in[...] = low[...].astype(F32).reshape(512, TILE).T
+    grad_out[...] = full[...].astype(F32).reshape(grad_out.shape)
+    grad_in[...] = low[...].astype(F32).reshape(grad_in.shape[::-1]).T
 
 
 def per_device(
     tile_values, tile_rows, tile_cols, tile_counts, features, weight_in, weight_out, cotangent
 ):
-    vmem = pl.BlockSpec(memory_space=pltpu.VMEM)
     hbm = pl.BlockSpec(memory_space=pltpu.HBM)
     block = pltpu.VMEM((BLOCKS, TILE, TILE), BF)
     dma = pltpu.SemaphoreType.DMA
@@ -622,8 +621,17 @@
             jax.ShapeDtypeStruct((TILE, 512), F32),
             jax.ShapeDtypeStruct((512, 512), F32),
         ),
-        in_specs=[vmem] * 3,
-        out_specs=(vmem, vmem, vmem),
+        grid=(2,),
+        in_specs=[
+            pl.BlockSpec((128, 512), lambda i: (i, 0)),
+            pl.BlockSpec((SHARE, CHUNK, WIDE), lambda i: (i, 0, 0)),
+            pl.BlockSpec((SHARE, CHUNK, TILE), lambda i: (i, 0, 0)),
+        ],
+        out_specs=(
+            pl.BlockSpec((128, 512), lambda i: (i, 0)),
+            pl.BlockSpec((TILE, 256), lambda i: (0, i)),
+            pl.BlockSpec((256, WIDE), lambda i: (i, 0)),
+        ),
         compiler_params=pltpu.CompilerParams(vmem_limit_bytes=60 * 1024 * 1024),
     )(logits, full, low)
 

time: 97 us -> 96.9 us (level)
  no operation moved by 1% of the time
where the time goes in v8:
time: 96.9 us; the launch traced here: 96.7 us
  Pallas kernels  96.1 us (99%)
    pallas_call x1, Pallas kernels, per_device(): pl.pallas_call(kernel, out_shape=(jax.ShapeDtypeStruct((256, 512), BF), j...  93.9 us
    pallas_call x1, Pallas kernels, per_device(): pl.pallas_call(unpack, out_shape=(jax.ShapeDtypeStruct((256, 512), BF), j...  2.2 us

profile of v8, /device:TPU:1, one launch (start us, length us, event | category | flops | bytes accessed | tf_op | source)
XLA Modules:
  0.0 96.7 jit_solution(12115295484566668031)
XLA Ops:
  0.6 93.9 %shard_map.103 = (bf16[256,512]{1,0:T(8,128)(2,1)}, bf16[32,16,512]{2,1,0:T(8,128)(2,1)}, bf16[32,16,128]{2,1,0:T(8,128)(2,1)}) custom-call(bf16[32,2,128,128]{3,2,1,0:T(8,128)(2,1)} %bitcast.9, s32[2,32]{1,0:T(2,128)} %bitcast.11, s32[2,32]{1,0:T(2,128)} %bitcast.12, s32[1,32]{1,0:T(1,128)} %bitcast.13, bf16[2,128,128]{2,1,0:T(8,128)(2,1)} %bitcast.10, ...), custom_call_target="tpu_custom_call" | custom-call | flops 5000000000 | bytes 5000000 | tf_op jit(solution)/shard_map/pallas_call | solution.py:591
  94.5 2.2 %shard_map.104 = (bf16[256,512]{1,0:T(8,128)(2,1)}, f32[128,512]{1,0:T(8,128)}, f32[512,512]{1,0:T(8,128)}) custom-call(bf16[256,512]{1,0:T(8,128)(2,1)} %get-tuple-element.6.logits_in, bf16[32,16,512]{2,1,0:T(8,128)(2,1)} %get-tuple-element.7.full, bf16[32,16,128]{2,1,0:T(8,128)(2,1)} %get-tuple-element.8.low), custom_call_target="tpu_custom_call" | custom-call | tf_op jit(solution)/shard_map/pallas_call | solution.py:617
